TPU v7x, 32 devices: a whole 2x2x4 slice. The times are simulated.
32 devices in a mesh: groups: 2 (over x), sector: 16 (over z, y, core).
Axes of the slice: x: 2, y: 2, z: 4, core: 2. Of those that a mesh axis runs over, the one named last changes fastest.
Arguments:
- field: float32 [4, 8, 64, 256], P('groups', None, 'sector'), parts along dimension 0, may hold values from -6 to 6
- source: float32 [4, 8, 64, 256], P('groups', None, 'sector'), parts along dimension 0, may hold values from -6 to 6
- materials: int32 [4, 8, 64, 256], P('groups', None, 'sector'), parts along dimension 0, may hold values from 0 to 3
- incoming: float32 [4, 4, 64, 256], P('groups', None, 'sector'), parts along dimension 0, may hold values from -6 to 6
- waveform: float32 [8], P('groups'), parts along dimension 0, may hold values from -1 to 1
- degrees: int32 [8], P('groups'), parts along dimension 0, may hold values from 4 to 8, as said below
- offsets: int32 [8], P('groups'), parts along dimension 0, may hold values from 0 to 15
- conduct: float32 [4], replicated, may hold values from 0.05 to 0.5
- reluct: float32 [4], replicated, may hold values from 0.3 to 3
- robin: float32 [2], replicated, may hold values from 0.5 to 2
Outputs:
- field_end: float32 [4, 8, 64, 256], P('groups', None, 'sector'), parts along dimension 0
- next_incoming: float32 [4, 4, 64, 256], P('groups', None, 'sector'), parts along dimension 0
There are 2 independent parts, one for each index of `groups`. A program takes and returns all parts, laid end to end along the dimension named above; an argument that names none is the same for every part. Nothing has to cross between parts.
Inputs may be any that keep to these rules, and one draw needn't show every extreme that they name: `degrees`: some step of each window has degree 8.
All inputs are finite; a program needn't handle non-finite values.
Results may differ from a plain program's by a relative error of at most 0.000021.
Values sent between devices are 32-bit elements; how exact they have to be, the bound alone decides.
A program may use at most 64 MiB of HBM per device.

v0:
```python
import jax
import jax.numpy as jnp
from jax import lax
from jax.sharding import PartitionSpec as P

DEG = 8


THETA = 1.05
DELTA = 0.95


def padded(value, sides, width):
    for axis, dim in sides:
        size, length = (lax.axis_size(axis), value.shape[dim])
        up = [(i, (i + 1) % size) for i in range(size)]
        down = [(j, i) for i, j in up]
        last = lax.slice_in_dim(value, length - width, length, axis=dim)
        first = lax.slice_in_dim(value, 0, width, axis=dim)
        before = lax.ppermute(last, axis, up)
        after = lax.ppermute(first, axis, down)
        value = jnp.concatenate([before, value, after], axis=dim)
    return value


def rates(count):
    rho = DELTA / THETA
    first = []
    second = []
    for step in range(count):
        fresh = 1.0 / (2.0 * THETA / DELTA - rho)
        first.append(fresh * rho)
        second.append(2.0 * fresh / DELTA)
        rho = fresh
    return (first, second)


def lookup(mats, table):
    result = jnp.zeros(mats.shape, jnp.float32)
    for index in range(table.shape[0]):
        result = result + jnp.where(mats == index, table[index], 0.0)
    return result


def centre(values, width):
    start = (values.shape[2] - width) // 2
    return values[:, :, start : start + width]


def coefs(nu_ext, sig, robin):
    nu_c = nu_ext[:, :, 1:-1]
    ka_p = 0.5 * (nu_c + nu_ext[:, :, 2:])
    ka_m = 0.5 * (nu_c + nu_ext[:, :, :-2])
    kr_in = 0.5 * (nu_c[:, :-1] + nu_c[:, 1:])
    zero_r = jnp.zeros_like(nu_c[:, :1])
    kr_p = jnp.concatenate([kr_in, zero_r], 1)
    kr_m = jnp.concatenate([zero_r, kr_in], 1)
    kz_in = 0.5 * (nu_c[..., :-1] + nu_c[..., 1:])
    zero_z = jnp.zeros_like(nu_c[..., :1])
    kz_p = jnp.concatenate([kz_in, zero_z], 3)
    kz_m = jnp.concatenate([zero_z, kz_in], 3)
    rpos = lax.broadcasted_iota(jnp.int32, nu_c.shape, 1)
    zpos = lax.broadcasted_iota(jnp.int32, nu_c.shape, 3)
    border = jnp.where(rpos == 0, nu_c, 0.0) + jnp.where(zpos == 0, nu_c, 0.0)
    border = border + jnp.where(zpos == nu_c.shape[3] - 1, nu_c, 0.0)
    border = border + jnp.where(rpos == nu_c.shape[1] - 1, robin[:, None, None, None], 0.0)
    diag = sig + ka_p + ka_m + kr_p + kr_m + kz_p + kz_m + border
    return (ka_p, ka_m, kr_p, kr_m, kz_p, kz_m, diag, 1.0 / diag)


def operate(x_ext, coef):
    ka_p, ka_m, kr_p, kr_m, kz_p, kz_m, diag, dinv = coef
    x_c = x_ext[:, :, 1:-1]
    zero_r = jnp.zeros_like(x_c[:, :1])
    zero_z = jnp.zeros_like(x_c[..., :1])
    up_r = jnp.concatenate([x_c[:, 1:], zero_r], 1)
    down_r = jnp.concatenate([zero_r, x_c[:, :-1]], 1)
    up_z = jnp.concatenate([x_c[..., 1:], zero_z], 3)
    down_z = jnp.concatenate([zero_z, x_c[..., :-1]], 3)
    beside = ka_p * x_ext[:, :, 2:] + ka_m * x_ext[:, :, :-2] + kr_p * up_r + kr_m * down_r
    beside = beside + kz_p * up_z + kz_m * down_z
    return diag * x_c - beside


def per_device(
    field, source, materials, incoming, waveform, degrees, offsets, conduct, reluct, robin
):
    cells = field.shape[2]
    layer = field.shape[1] - 1
    steps = incoming.shape[1]
    nu = lookup(materials, reluct)
    sig = lookup(materials, conduct)
    depth = 1
    wide = cells + 2 * (depth - 1)
    both_ext = padded(jnp.stack([nu, sig]), (("sector", 3),), depth)
    coef_wide = coefs(both_ext[0], centre(both_ext[1], wide), robin)
    coef_mid = tuple((centre(part_c, cells) for part_c in coef_wide))
    first, second = rates(DEG)
    state = field
    traces = []
    for step in range(steps):
        rhs = sig * state + waveform[step] * source
        rhs = rhs.at[:, layer].add(incoming[:, step])
        iterate = state
        state_ext = padded(iterate, (("sector", 2),), 1)
        resid = rhs - operate(state_ext, coef_mid)
        direction = coef_mid[7] * resid * (1.0 / THETA)
        for block in range(DEG // depth):
            direction_w = padded(direction, (("sector", 2),), 1)
            resid_w = resid
            sweep = block * depth
            width = direction_w.shape[2] - 2
            coef = tuple((centre(part_c, width) for part_c in coef_wide))
            active = (sweep < degrees[step]).astype(jnp.float32)
            iterate = iterate + active * centre(direction_w, cells)
            resid_w = centre(resid_w, width) - operate(direction_w, coef)
            direction_w = first[sweep] * centre(direction_w, width) + second[sweep] * (
                coef[7] * resid_w
            )
            resid = resid_w
            direction = direction_w
        state = iterate
        traces.append(2.0 * robin[:, None, None] * state[:, layer] - incoming[:, step])
    outgoing = jnp.stack(traces, 1)
    count = lax.axis_size("sector")
    whole = lax.all_gather(outgoing, "sector", axis=2, tiled=True)
    place = lax.axis_index("sector")
    rotor_new = []
    stator_new = []
    for step in range(steps):
        from_rotor = (place - offsets[step]) % count * cells
        from_stator = (place + offsets[step]) % count * cells
        stator_new.append(lax.dynamic_slice_in_dim(whole[0, step], from_rotor, cells, 0))
        rotor_new.append(lax.dynamic_slice_in_dim(whole[1, step], from_stator, cells, 0))
    next_incoming = jnp.stack([jnp.stack(rotor_new), jnp.stack(stator_new)])
    return (state, next_incoming)


def solution(mesh):
    return jax.shard_map(
        per_device,
        mesh=mesh,
        in_specs=(
            P("groups", None, "sector", None),
            P("groups", None, "sector", None),
            P("groups", None, "sector", None),
            P("groups", None, "sector", None),
            P("groups"),
            P("groups"),
            P("groups"),
            P(),
            P(),
            P(),
        ),
        out_specs=(P("groups", None, "sector", None), P("groups", None, "sector", None)),
        check_vma=False,
    )
```

profile of v0, /device:TPU:0, one launch (start us, length us, event | category | flops | bytes accessed | tf_op | source)
XLA Modules:
  0.0 287.5 jit_solution(17153086395063980901)
XLA Ops:
  0.6 1.5 fusion.452
  3.4 3.9 %multiply_add_fusion.20 = (f32[2,8,4,256]{3,1,0,2:T(8,128)S(1)}, pred[2,8,4,256]{3,1,0,2:T(8,128)(4,1)S(1)}, pred[2,8,4,256]{3,1,0,2:T(8,128)(4,1)S(1)}, pred[2,...) fusion(f32[2,8,4,256]{3,2,1,0:T(4,128)} %param.19, f32[]{:T(128)} %bitcast.12, ...), kind=kLoop, calls=%fused_computation.439 | loop fusion | flops 229376 | bytes 393236 | tf_op jit(solution)/shard_map/add | solution.py:102
  7.4 4.9 %add_bitcast_fusion = (f32[1,2,8,4,256]{4,2,1,3,0:T(8,128)S(1)}, f32[1,2,8,4,256]{4,2,1,3,0:T(8,128)S(1)}) fusion(pred[2,8,4,256]{3,1,0,2:T(8,128)(4,1)S(1)} %get-tuple-element.73, pred[2,8,4,256]{3,1,0,2:T(8,128)(4,1)S(1)} %get-tuple-element.72, pred[2,8,4,256]{3,1,0,2:T(8,128)(4,1)S(1)} %get-tuple-element.71, ...), kind=kLoop, calls=%fused_computation.441 | loop fusion | flops 229376 | bytes 196640 | tf_op jit(solution)/shard_map/stack | solution.py:95
  12.2 5.5 %collective-permute-start.1 = (f32[2,2,8,1,256]{4,2,1,3,0:T(8,128)S(1)}, f32[2,2,8,1,256]{4,2,1,3,0:T(8,128)S(1)}, u32[]{:S(2)}, u32[]{:S(2)}) collective-permute-start(f32[2,2,8,1,256]{4,2,1,3,0:T(8,128)S(1)} %get-tuple-element.85), channel_id=1, source_target_pairs={{1,0},{2,1},{3,2},{4,3},{5,4},{6,5},{7,6},{8,7},{9,8},{10,9},{11,1... | collective-permute-start | bytes 98312 | tf_op jit(solution)/shard_map/ppermute | solution.py:21
  17.8 4.5 %collective-permute-start.2 = (f32[2,8,1,256]{3,1,0,2:T(8,128)S(1)}, f32[2,8,1,256]{3,1,0,2:T(8,128)S(1)}, u32[]{:S(2)}, u32[]{:S(2)}) collective-permute-start(f32[2,8,1,256]{3,1,0,2:T(8,128)S(1)} %get-tuple-element.272), channel_id=1, source_target_pairs={{1,0},{2,1},{3,2},{4,3},{5,4},{6,5},{7,6},{8,7},{9,8},{10,9},{11,1... | collective-permute-start | bytes 49160 | tf_op jit(solution)/shard_map/ppermute | solution.py:21
  52.1 4.4 %collective-permute-start.4 = (f32[2,8,1,256]{3,1,0,2:T(8,128)S(1)}, f32[2,8,1,256]{3,1,0,2:T(8,128)S(1)}, u32[]{:S(2)}, u32[]{:S(2)}) collective-permute-start(f32[2,8,1,256]{3,1,0,2:T(8,128)S(1)} %get-tuple-element.266), channel_id=1, source_target_pairs={{1,0},{2,1},{3,2},{4,3},{5,4},{6,5},{7,6},{8,7},{9,8},{10,9},{11,1... | collective-permute-start | bytes 49160 | tf_op jit(solution)/shard_map/ppermute | solution.py:21
  56.5 1.4 collective-permute-done.5
  58.2 4.5 %collective-permute-start.6 = (f32[2,8,1,256]{3,1,0,2:T(8,128)S(1)}, f32[2,8,1,256]{3,1,0,2:T(8,128)S(1)}, u32[]{:S(2)}, u32[]{:S(2)}) collective-permute-start(f32[2,8,1,256]{3,1,0,2:T(8,128)S(1)} %get-tuple-element.260), channel_id=1, source_target_pairs={{1,0},{2,1},{3,2},{4,3},{5,4},{6,5},{7,6},{8,7},{9,8},{10,9},{11,1... | collective-permute-start | bytes 49160 | tf_op jit(solution)/shard_map/ppermute | solution.py:21
  62.7 1.4 collective-permute-done.7
  64.5 4.5 %collective-permute-start.8 = (f32[2,8,1,256]{3,1,0,2:T(8,128)S(1)}, f32[2,8,1,256]{3,1,0,2:T(8,128)S(1)}, u32[]{:S(2)}, u32[]{:S(2)}) collective-permute-start(f32[2,8,1,256]{3,1,0,2:T(8,128)S(1)} %get-tuple-element.254), channel_id=1, source_target_pairs={{1,0},{2,1},{3,2},{4,3},{5,4},{6,5},{7,6},{8,7},{9,8},{10,9},{11,1... | collective-permute-start | bytes 49160 | tf_op jit(solution)/shard_map/ppermute | solution.py:21
  69.0 1.4 collective-permute-done.9
  70.8 4.5 %collective-permute-start.10 = (f32[2,8,1,256]{3,1,0,2:T(8,128)S(1)}, f32[2,8,1,256]{3,1,0,2:T(8,128)S(1)}, u32[]{:S(2)}, u32[]{:S(2)}) collective-permute-start(f32[2,8,1,256]{3,1,0,2:T(8,128)S(1)} %get-tuple-element.248), channel_id=1, source_target_pairs={{1,0},{2,1},{3,2},{4,3},{5,4},{6,5},{7,6},{8,7},{9,8},{10,9},{11,1... | collective-permute-start | bytes 49160 | tf_op jit(solution)/shard_map/ppermute | solution.py:21
  75.2 1.4 collective-permute-done.11
  77.0 4.5 %collective-permute-start.12 = (f32[2,8,1,256]{3,1,0,2:T(8,128)S(1)}, f32[2,8,1,256]{3,1,0,2:T(8,128)S(1)}, u32[]{:S(2)}, u32[]{:S(2)}) collective-permute-start(f32[2,8,1,256]{3,1,0,2:T(8,128)S(1)} %get-tuple-element.242), channel_id=1, source_target_pairs={{1,0},{2,1},{3,2},{4,3},{5,4},{6,5},{7,6},{8,7},{9,8},{10,9},{11,1... | collective-permute-start | bytes 49160 | tf_op jit(solution)/shard_map/ppermute | solution.py:21
  81.4 1.4 collective-permute-done.13
  83.2 4.5 %collective-permute-start.14 = (f32[2,8,1,256]{3,1,0,2:T(8,128)S(1)}, f32[2,8,1,256]{3,1,0,2:T(8,128)S(1)}, u32[]{:S(2)}, u32[]{:S(2)}) collective-permute-start(f32[2,8,1,256]{3,1,0,2:T(8,128)S(1)} %get-tuple-element.236), channel_id=1, source_target_pairs={{1,0},{2,1},{3,2},{4,3},{5,4},{6,5},{7,6},{8,7},{9,8},{10,9},{11,1... | collective-permute-start | bytes 49160 | tf_op jit(solution)/shard_map/ppermute | solution.py:21
  87.7 1.4 collective-permute-done.15
  89.5 4.5 %collective-permute-start.16 = (f32[2,8,1,256]{3,1,0,2:T(8,128)S(1)}, f32[2,8,1,256]{3,1,0,2:T(8,128)S(1)}, u32[]{:S(2)}, u32[]{:S(2)}) collective-permute-start(f32[2,8,1,256]{3,1,0,2:T(8,128)S(1)} %get-tuple-element.230), channel_id=1, source_target_pairs={{1,0},{2,1},{3,2},{4,3},{5,4},{6,5},{7,6},{8,7},{9,8},{10,9},{11,1... | collective-permute-start | bytes 49160 | tf_op jit(solution)/shard_map/ppermute | solution.py:21
  94.0 1.4 collective-permute-done.17
  95.4 3.4 %multiply_add_fusion.19 = (f32[2,8,4,256]{3,1,0,2:T(8,128)S(1)}, f32[2,8,4,256]{3,1,0,2:T(8,128)S(1)}) fusion(f32[2,8,4,256]{3,2,1,0:T(4,128)S(1)} %copy-done.87, f32[]{:T(128)} %bitcast.21, pred[2,8,4,256]{3,1,0,2:T(8,128)(4,1)S(1)} %get-tuple-element.73, f32[]{:T(128)} %bitcast.8, pred[2,8,4,256]{3,1,0,2:T(8,128)(4,1)S(1)} %get-tuple-element.72, ...), kind=kLoop, calls=%fused_computation.438 | loop fusion | flops 2097152 | bytes 2561332 | tf_op jit(solution)/shard_map/add | solution.py:102
  99.0 4.5 %collective-permute-start.18 = (f32[2,8,1,256]{3,1,0,2:T(8,128)S(1)}, f32[2,8,1,256]{3,1,0,2:T(8,128)S(1)}, u32[]{:S(2)}, u32[]{:S(2)}) collective-permute-start(f32[2,8,1,256]{3,1,0,2:T(8,128)S(1)} %get-tuple-element.224), channel_id=1, source_target_pairs={{1,0},{2,1},{3,2},{4,3},{5,4},{6,5},{7,6},{8,7},{9,8},{10,9},{11,1... | collective-permute-start | bytes 49160 | tf_op jit(solution)/shard_map/ppermute | solution.py:21
  105.1 4.5 %collective-permute-start.20 = (f32[2,8,1,256]{3,1,0,2:T(8,128)S(1)}, f32[2,8,1,256]{3,1,0,2:T(8,128)S(1)}, u32[]{:S(2)}, u32[]{:S(2)}) collective-permute-start(f32[2,8,1,256]{3,1,0,2:T(8,128)S(1)} %get-tuple-element.218), channel_id=1, source_target_pairs={{1,0},{2,1},{3,2},{4,3},{5,4},{6,5},{7,6},{8,7},{9,8},{10,9},{11,1... | collective-permute-start | bytes 49160 | tf_op jit(solution)/shard_map/ppermute | solution.py:21
  109.6 1.4 collective-permute-done.21
  111.3 4.5 %collective-permute-start.22 = (f32[2,8,1,256]{3,1,0,2:T(8,128)S(1)}, f32[2,8,1,256]{3,1,0,2:T(8,128)S(1)}, u32[]{:S(2)}, u32[]{:S(2)}) collective-permute-start(f32[2,8,1,256]{3,1,0,2:T(8,128)S(1)} %get-tuple-element.212), channel_id=1, source_target_pairs={{1,0},{2,1},{3,2},{4,3},{5,4},{6,5},{7,6},{8,7},{9,8},{10,9},{11,1... | collective-permute-start | bytes 49160 | tf_op jit(solution)/shard_map/ppermute | solution.py:21
  115.8 1.4 collective-permute-done.23
  117.6 4.5 %collective-permute-start.24 = (f32[2,8,1,256]{3,1,0,2:T(8,128)S(1)}, f32[2,8,1,256]{3,1,0,2:T(8,128)S(1)}, u32[]{:S(2)}, u32[]{:S(2)}) collective-permute-start(f32[2,8,1,256]{3,1,0,2:T(8,128)S(1)} %get-tuple-element.206), channel_id=1, source_target_pairs={{1,0},{2,1},{3,2},{4,3},{5,4},{6,5},{7,6},{8,7},{9,8},{10,9},{11,1... | collective-permute-start | bytes 49160 | tf_op jit(solution)/shard_map/ppermute | solution.py:21
  122.1 1.4 collective-permute-done.25
  123.9 4.5 %collective-permute-start.26 = (f32[2,8,1,256]{3,1,0,2:T(8,128)S(1)}, f32[2,8,1,256]{3,1,0,2:T(8,128)S(1)}, u32[]{:S(2)}, u32[]{:S(2)}) collective-permute-start(f32[2,8,1,256]{3,1,0,2:T(8,128)S(1)} %get-tuple-element.200), channel_id=1, source_target_pairs={{1,0},{2,1},{3,2},{4,3},{5,4},{6,5},{7,6},{8,7},{9,8},{10,9},{11,1... | collective-permute-start | bytes 49160 | tf_op jit(solution)/shard_map/ppermute | solution.py:21
  128.4 1.4 collective-permute-done.27
  130.2 4.5 %collective-permute-start.28 = (f32[2,8,1,256]{3,1,0,2:T(8,128)S(1)}, f32[2,8,1,256]{3,1,0,2:T(8,128)S(1)}, u32[]{:S(2)}, u32[]{:S(2)}) collective-permute-start(f32[2,8,1,256]{3,1,0,2:T(8,128)S(1)} %get-tuple-element.194), channel_id=1, source_target_pairs={{1,0},{2,1},{3,2},{4,3},{5,4},{6,5},{7,6},{8,7},{9,8},{10,9},{11,1... | collective-permute-start | bytes 49160 | tf_op jit(solution)/shard_map/ppermute | solution.py:21
  134.7 1.4 collective-permute-done.29
  136.6 4.5 %collective-permute-start.30 = (f32[2,8,1,256]{3,1,0,2:T(8,128)S(1)}, f32[2,8,1,256]{3,1,0,2:T(8,128)S(1)}, u32[]{:S(2)}, u32[]{:S(2)}) collective-permute-start(f32[2,8,1,256]{3,1,0,2:T(8,128)S(1)} %get-tuple-element.188), channel_id=1, source_target_pairs={{1,0},{2,1},{3,2},{4,3},{5,4},{6,5},{7,6},{8,7},{9,8},{10,9},{11,1... | collective-permute-start | bytes 49160 | tf_op jit(solution)/shard_map/ppermute | solution.py:21
  141.1 1.3 collective-permute-done.31
  143.1 4.5 %collective-permute-start.32 = (f32[2,8,1,256]{3,1,0,2:T(8,128)S(1)}, f32[2,8,1,256]{3,1,0,2:T(8,128)S(1)}, u32[]{:S(2)}, u32[]{:S(2)}) collective-permute-start(f32[2,8,1,256]{3,1,0,2:T(8,128)S(1)} %get-tuple-element.182), channel_id=1, source_target_pairs={{1,0},{2,1},{3,2},{4,3},{5,4},{6,5},{7,6},{8,7},{9,8},{10,9},{11,1... | collective-permute-start | bytes 49160 | tf_op jit(solution)/shard_map/ppermute | solution.py:21
  149.7 4.5 %collective-permute-start.34 = (f32[2,8,1,256]{3,1,0,2:T(8,128)S(1)}, f32[2,8,1,256]{3,1,0,2:T(8,128)S(1)}, u32[]{:S(2)}, u32[]{:S(2)}) collective-permute-start(f32[2,8,1,256]{3,1,0,2:T(8,128)S(1)} %get-tuple-element.176), channel_id=1, source_target_pairs={{1,0},{2,1},{3,2},{4,3},{5,4},{6,5},{7,6},{8,7},{9,8},{10,9},{11,1... | collective-permute-start | bytes 49160 | tf_op jit(solution)/shard_map/ppermute | solution.py:21
  154.4 3.5 %multiply_add_fusion.13 = f32[2,8,4,256]{3,1,0,2:T(8,128)S(1)} fusion(f32[2,8,4,255]{3,1,0,2:T(8,128)S(1)} %get-tuple-element.187, f32[2,8,4,255]{3,1,0,2:T(8,128)S(1)} %get-tuple-element.186, f32[2,7,4,256]{3,1,0,2:T(8,128)S(1)} %get-tuple-element.185, f32[2,7,4,256]{3,1,0,2:T(8,128)S(1)} %get-tuple-element.184, ...), kind=kLoop, calls=%fused_computation.403 | loop fusion | flops 2686976 | bytes 3051828 | tf_op jit(solution)/shard_map/add | solution.py:102
  158.3 4.4 %collective-permute-start.36 = (f32[2,8,1,256]{3,1,0,2:T(8,128)S(1)}, f32[2,8,1,256]{3,1,0,2:T(8,128)S(1)}, u32[]{:S(2)}, u32[]{:S(2)}) collective-permute-start(f32[2,8,1,256]{3,1,0,2:T(8,128)S(1)} %get-tuple-element.170), channel_id=1, source_target_pairs={{1,0},{2,1},{3,2},{4,3},{5,4},{6,5},{7,6},{8,7},{9,8},{10,9},{11,1... | collective-permute-start | bytes 49160 | tf_op jit(solution)/shard_map/ppermute | solution.py:21
  162.7 1.4 collective-permute-done.37
  164.4 4.5 %collective-permute-start.38 = (f32[2,8,1,256]{3,1,0,2:T(8,128)S(1)}, f32[2,8,1,256]{3,1,0,2:T(8,128)S(1)}, u32[]{:S(2)}, u32[]{:S(2)}) collective-permute-start(f32[2,8,1,256]{3,1,0,2:T(8,128)S(1)} %get-tuple-element.164), channel_id=1, source_target_pairs={{1,0},{2,1},{3,2},{4,3},{5,4},{6,5},{7,6},{8,7},{9,8},{10,9},{11,1... | collective-permute-start | bytes 49160 | tf_op jit(solution)/shard_map/ppermute | solution.py:21
  168.9 1.4 collective-permute-done.39
  170.7 4.7 %collective-permute-start.40 = (f32[2,8,1,256]{3,1,0,2:T(8,128)S(1)}, f32[2,8,1,256]{3,1,0,2:T(8,128)S(1)}, u32[]{:S(2)}, u32[]{:S(2)}) collective-permute-start(f32[2,8,1,256]{3,1,0,2:T(8,128)S(1)} %get-tuple-element.158), channel_id=1, source_target_pairs={{1,0},{2,1},{3,2},{4,3},{5,4},{6,5},{7,6},{8,7},{9,8},{10,9},{11,1... | collective-permute-start | bytes 49160 | tf_op jit(solution)/shard_map/ppermute | solution.py:21
  177.1 4.5 %collective-permute-start.42 = (f32[2,8,1,256]{3,1,0,2:T(8,128)S(1)}, f32[2,8,1,256]{3,1,0,2:T(8,128)S(1)}, u32[]{:S(2)}, u32[]{:S(2)}) collective-permute-start(f32[2,8,1,256]{3,1,0,2:T(8,128)S(1)} %get-tuple-element.152), channel_id=1, source_target_pairs={{1,0},{2,1},{3,2},{4,3},{5,4},{6,5},{7,6},{8,7},{9,8},{10,9},{11,1... | collective-permute-start | bytes 49160 | tf_op jit(solution)/shard_map/ppermute | solution.py:21
  183.5 4.5 %collective-permute-start.44 = (f32[2,8,1,256]{3,1,0,2:T(8,128)S(1)}, f32[2,8,1,256]{3,1,0,2:T(8,128)S(1)}, u32[]{:S(2)}, u32[]{:S(2)}) collective-permute-start(f32[2,8,1,256]{3,1,0,2:T(8,128)S(1)} %get-tuple-element.146), channel_id=1, source_target_pairs={{1,0},{2,1},{3,2},{4,3},{5,4},{6,5},{7,6},{8,7},{9,8},{10,9},{11,1... | collective-permute-start | bytes 49160 | tf_op jit(solution)/shard_map/ppermute | solution.py:21
  188.0 1.3 collective-permute-done.45
  189.9 4.5 %collective-permute-start.46 = (f32[2,8,1,256]{3,1,0,2:T(8,128)S(1)}, f32[2,8,1,256]{3,1,0,2:T(8,128)S(1)}, u32[]{:S(2)}, u32[]{:S(2)}) collective-permute-start(f32[2,8,1,256]{3,1,0,2:T(8,128)S(1)} %get-tuple-element.140), channel_id=1, source_target_pairs={{1,0},{2,1},{3,2},{4,3},{5,4},{6,5},{7,6},{8,7},{9,8},{10,9},{11,1... | collective-permute-start | bytes 49160 | tf_op jit(solution)/shard_map/ppermute | solution.py:21
  196.5 4.5 %collective-permute-start.48 = (f32[2,8,1,256]{3,1,0,2:T(8,128)S(1)}, f32[2,8,1,256]{3,1,0,2:T(8,128)S(1)}, u32[]{:S(2)}, u32[]{:S(2)}) collective-permute-start(f32[2,8,1,256]{3,1,0,2:T(8,128)S(1)} %get-tuple-element.134), channel_id=1, source_target_pairs={{1,0},{2,1},{3,2},{4,3},{5,4},{6,5},{7,6},{8,7},{9,8},{10,9},{11,1... | collective-permute-start | bytes 49160 | tf_op jit(solution)/shard_map/ppermute | solution.py:21
  205.6 4.4 %collective-permute-start.50 = (f32[2,8,1,256]{3,1,0,2:T(8,128)}, f32[2,8,1,256]{3,1,0,2:T(8,128)}, u32[]{:S(2)}, u32[]{:S(2)}) collective-permute-start(f32[2,8,1,256]{3,1,0,2:T(8,128)} %get-tuple-element.128), channel_id=1, source_target_pairs={{1,0},{2,1},{3,2},{4,3},{5,4},{6,5},{7,6},{8,7},{9,8},{10,9},{11,1... | collective-permute-start | bytes 49160 | tf_op jit(solution)/shard_map/ppermute | solution.py:21
  210.4 3.9 %multiply_add_fusion.6 = f32[2,8,4,256]{3,1,0,2:T(8,128)S(1)} fusion(f32[2,8,4,255]{3,1,0,2:T(8,128)S(1)} %get-tuple-element.139, f32[2,8,4,255]{3,1,0,2:T(8,128)S(1)} %get-tuple-element.138, f32[2,7,4,256]{3,1,0,2:T(8,128)S(1)} %get-tuple-element.137, f32[2,7,4,256]{3,1,0,2:T(8,128)S(1)} %get-tuple-element.136, f32[2,8,4,256]{3,1,0,2:T(8,128)S(1)} %get-tuple-element.68, ...), kind=kLoop, calls=%fused_computation.396 | loop fusion | flops 5128192 | bytes 5522260 | tf_op jit(solution)/shard_map/add | solution.py:102
  215.6 1.5 scatter-add.19
  218.4 4.4 %collective-permute-start.52 = (f32[2,8,1,256]{3,1,0,2:T(8,128)S(1)}, f32[2,8,1,256]{3,1,0,2:T(8,128)S(1)}, u32[]{:S(2)}, u32[]{:S(2)}) collective-permute-start(f32[2,8,1,256]{3,1,0,2:T(8,128)S(1)} %get-tuple-element.122), channel_id=1, source_target_pairs={{1,0},{2,1},{3,2},{4,3},{5,4},{6,5},{7,6},{8,7},{9,8},{10,9},{11,1... | collective-permute-start | bytes 49160 | tf_op jit(solution)/shard_map/ppermute | solution.py:21
  222.8 1.4 collective-permute-done.53
  224.5 4.5 %collective-permute-start.54 = (f32[2,8,1,256]{3,1,0,2:T(8,128)S(1)}, f32[2,8,1,256]{3,1,0,2:T(8,128)S(1)}, u32[]{:S(2)}, u32[]{:S(2)}) collective-permute-start(f32[2,8,1,256]{3,1,0,2:T(8,128)S(1)} %get-tuple-element.116), channel_id=1, source_target_pairs={{1,0},{2,1},{3,2},{4,3},{5,4},{6,5},{7,6},{8,7},{9,8},{10,9},{11,1... | collective-permute-start | bytes 49160 | tf_op jit(solution)/shard_map/ppermute | solution.py:21
  229.0 1.4 collective-permute-done.55
  230.7 4.5 %collective-permute-start.56 = (f32[2,8,1,256]{3,1,0,2:T(8,128)S(1)}, f32[2,8,1,256]{3,1,0,2:T(8,128)S(1)}, u32[]{:S(2)}, u32[]{:S(2)}) collective-permute-start(f32[2,8,1,256]{3,1,0,2:T(8,128)S(1)} %get-tuple-element.110), channel_id=1, source_target_pairs={{1,0},{2,1},{3,2},{4,3},{5,4},{6,5},{7,6},{8,7},{9,8},{10,9},{11,1... | collective-permute-start | bytes 49160 | tf_op jit(solution)/shard_map/ppermute | solution.py:21
  235.2 1.4 collective-permute-done.57
  237.0 4.5 %collective-permute-start.58 = (f32[2,8,1,256]{3,1,0,2:T(8,128)S(1)}, f32[2,8,1,256]{3,1,0,2:T(8,128)S(1)}, u32[]{:S(2)}, u32[]{:S(2)}) collective-permute-start(f32[2,8,1,256]{3,1,0,2:T(8,128)S(1)} %get-tuple-element.104), channel_id=1, source_target_pairs={{1,0},{2,1},{3,2},{4,3},{5,4},{6,5},{7,6},{8,7},{9,8},{10,9},{11,1... | collective-permute-start | bytes 49160 | tf_op jit(solution)/shard_map/ppermute | solution.py:21
  241.5 1.4 collective-permute-done.59
  243.2 4.5 %collective-permute-start.60 = (f32[2,8,1,256]{3,1,0,2:T(8,128)S(1)}, f32[2,8,1,256]{3,1,0,2:T(8,128)S(1)}, u32[]{:S(2)}, u32[]{:S(2)}) collective-permute-start(f32[2,8,1,256]{3,1,0,2:T(8,128)S(1)} %get-tuple-element.98), channel_id=1, source_target_pairs={{1,0},{2,1},{3,2},{4,3},{5,4},{6,5},{7,6},{8,7},{9,8},{10,9},{11,1... | collective-permute-start | bytes 49160 | tf_op jit(solution)/shard_map/ppermute | solution.py:21
  247.7 1.4 collective-permute-done.61
  249.5 4.5 %collective-permute-start.62 = (f32[2,8,1,256]{3,1,0,2:T(8,128)S(1)}, f32[2,8,1,256]{3,1,0,2:T(8,128)S(1)}, u32[]{:S(2)}, u32[]{:S(2)}) collective-permute-start(f32[2,8,1,256]{3,1,0,2:T(8,128)S(1)} %get-tuple-element.92), channel_id=1, source_target_pairs={{1,0},{2,1},{3,2},{4,3},{5,4},{6,5},{7,6},{8,7},{9,8},{10,9},{11,1... | collective-permute-start | bytes 49160 | tf_op jit(solution)/shard_map/ppermute | solution.py:21
  254.0 1.4 collective-permute-done.63
  256.1 4.5 %collective-permute-start.64 = (f32[2,8,1,256]{3,1,0,2:T(8,128)S(1)}, f32[2,8,1,256]{3,1,0,2:T(8,128)S(1)}, u32[]{:S(2)}, u32[]{:S(2)}) collective-permute-start(f32[2,8,1,256]{3,1,0,2:T(8,128)S(1)} %get-tuple-element.90), channel_id=1, source_target_pairs={{1,0},{2,1},{3,2},{4,3},{5,4},{6,5},{7,6},{8,7},{9,8},{10,9},{11,1... | collective-permute-start | bytes 49160 | tf_op jit(solution)/shard_map/ppermute | solution.py:21
  262.4 2.7 fusion.12
  266.8 19.4 %all_gather.3 = f32[2,4,64,256]{3,1,0,2:T(4,128)S(1)} all-gather(f32[2,4,4,256]{3,1,0,2:T(4,128)S(1)} %pad_maximum_fusion.67), channel_id=1, replica_groups=mesh['groups'=2,'sector'=16] {'sector'}, dimensions={2}, use_global_device_ids=true | all-gather | bytes 557056 | tf_op jit(solution)/shard_map/all_gather | solution.py:126
  (518 shorter events, 35.3 us)
Async XLA Ops:
  12.2 39.4 %collective-permute-start.1 = (f32[2,2,8,1,256]{4,2,1,3,0:T(8,128)S(1)}, f32[2,2,8,1,256]{4,2,1,3,0:T(8,128)S(1)}, u32[]{:S(2)}, u32[]{:S(2)}) collective-permute-start(f32[2,2,8,1,256]{4,2,1,3,0:T(8,128)S(1)} %get-tuple-element.85), channel_id=1, source_target_pairs={{1,0},{2,1},{3,2},{4,3},{5,4},{6,5},{7,6},{8,7},{9,8},{10,9},{11,1... | collective-permute-start | bytes 98312 | tf_op jit(solution)/shard_map/ppermute | solution.py:21
  17.7 33.9 %collective-permute-start = (f32[2,2,8,1,256]{4,2,1,3,0:T(8,128)S(1)}, f32[2,2,8,1,256]{4,2,1,3,0:T(8,128)S(1)}, u32[]{:S(2)}, u32[]{:S(2)}) collective-permute-start(f32[2,2,8,1,256]{4,2,1,3,0:T(8,128)S(1)} %get-tuple-element.84), channel_id=1, source_target_pairs={{0,1},{1,2},{2,3},{3,4},{4,5},{5,6},{6,7},{7,8},{8,9},{9,10},{10,1... | collective-permute-start | bytes 98312 | tf_op jit(solution)/shard_map/ppermute | solution.py:20
  17.8 34.0 %collective-permute-start.3 = (f32[2,8,1,256]{3,1,0,2:T(8,128)S(1)}, f32[2,8,1,256]{3,1,0,2:T(8,128)S(1)}, u32[]{:S(2)}, u32[]{:S(2)}) collective-permute-start(f32[2,8,1,256]{3,1,0,2:T(8,128)S(1)} %get-tuple-element.273), channel_id=1, source_target_pairs={{0,1},{1,2},{2,3},{3,4},{4,5},{5,6},{6,7},{7,8},{8,9},{9,10},{10,1... | collective-permute-start | bytes 49160 | tf_op jit(solution)/shard_map/ppermute | solution.py:20
  17.8 34.0 %collective-permute-start.2 = (f32[2,8,1,256]{3,1,0,2:T(8,128)S(1)}, f32[2,8,1,256]{3,1,0,2:T(8,128)S(1)}, u32[]{:S(2)}, u32[]{:S(2)}) collective-permute-start(f32[2,8,1,256]{3,1,0,2:T(8,128)S(1)} %get-tuple-element.272), channel_id=1, source_target_pairs={{1,0},{2,1},{3,2},{4,3},{5,4},{6,5},{7,6},{8,7},{9,8},{10,9},{11,1... | collective-permute-start | bytes 49160 | tf_op jit(solution)/shard_map/ppermute | solution.py:21
  52.0 5.9 %collective-permute-start.5 = (f32[2,8,1,256]{3,1,0,2:T(8,128)S(1)}, f32[2,8,1,256]{3,1,0,2:T(8,128)S(1)}, u32[]{:S(2)}, u32[]{:S(2)}) collective-permute-start(f32[2,8,1,256]{3,1,0,2:T(8,128)S(1)} %get-tuple-element.267), channel_id=1, source_target_pairs={{0,1},{1,2},{2,3},{3,4},{4,5},{5,6},{6,7},{7,8},{8,9},{9,10},{10,1... | collective-permute-start | bytes 49160 | tf_op jit(solution)/shard_map/ppermute | solution.py:20
  58.2 5.9 %collective-permute-start.7 = (f32[2,8,1,256]{3,1,0,2:T(8,128)S(1)}, f32[2,8,1,256]{3,1,0,2:T(8,128)S(1)}, u32[]{:S(2)}, u32[]{:S(2)}) collective-permute-start(f32[2,8,1,256]{3,1,0,2:T(8,128)S(1)} %get-tuple-element.261), channel_id=1, source_target_pairs={{0,1},{1,2},{2,3},{3,4},{4,5},{5,6},{6,7},{7,8},{8,9},{9,10},{10,1... | collective-permute-start | bytes 49160 | tf_op jit(solution)/shard_map/ppermute | solution.py:20
  58.2 5.9 %collective-permute-start.6 = (f32[2,8,1,256]{3,1,0,2:T(8,128)S(1)}, f32[2,8,1,256]{3,1,0,2:T(8,128)S(1)}, u32[]{:S(2)}, u32[]{:S(2)}) collective-permute-start(f32[2,8,1,256]{3,1,0,2:T(8,128)S(1)} %get-tuple-element.260), channel_id=1, source_target_pairs={{1,0},{2,1},{3,2},{4,3},{5,4},{6,5},{7,6},{8,7},{9,8},{10,9},{11,1... | collective-permute-start | bytes 49160 | tf_op jit(solution)/shard_map/ppermute | solution.py:21
  64.4 5.9 %collective-permute-start.9 = (f32[2,8,1,256]{3,1,0,2:T(8,128)S(1)}, f32[2,8,1,256]{3,1,0,2:T(8,128)S(1)}, u32[]{:S(2)}, u32[]{:S(2)}) collective-permute-start(f32[2,8,1,256]{3,1,0,2:T(8,128)S(1)} %get-tuple-element.255), channel_id=1, source_target_pairs={{0,1},{1,2},{2,3},{3,4},{4,5},{5,6},{6,7},{7,8},{8,9},{9,10},{10,1... | collective-permute-start | bytes 49160 | tf_op jit(solution)/shard_map/ppermute | solution.py:20
  64.5 5.9 %collective-permute-start.8 = (f32[2,8,1,256]{3,1,0,2:T(8,128)S(1)}, f32[2,8,1,256]{3,1,0,2:T(8,128)S(1)}, u32[]{:S(2)}, u32[]{:S(2)}) collective-permute-start(f32[2,8,1,256]{3,1,0,2:T(8,128)S(1)} %get-tuple-element.254), channel_id=1, source_target_pairs={{1,0},{2,1},{3,2},{4,3},{5,4},{6,5},{7,6},{8,7},{9,8},{10,9},{11,1... | collective-permute-start | bytes 49160 | tf_op jit(solution)/shard_map/ppermute | solution.py:21
  70.7 5.9 %collective-permute-start.11 = (f32[2,8,1,256]{3,1,0,2:T(8,128)S(1)}, f32[2,8,1,256]{3,1,0,2:T(8,128)S(1)}, u32[]{:S(2)}, u32[]{:S(2)}) collective-permute-start(f32[2,8,1,256]{3,1,0,2:T(8,128)S(1)} %get-tuple-element.249), channel_id=1, source_target_pairs={{0,1},{1,2},{2,3},{3,4},{4,5},{5,6},{6,7},{7,8},{8,9},{9,10},{10,1... | collective-permute-start | bytes 49160 | tf_op jit(solution)/shard_map/ppermute | solution.py:20
  70.8 5.9 %collective-permute-start.10 = (f32[2,8,1,256]{3,1,0,2:T(8,128)S(1)}, f32[2,8,1,256]{3,1,0,2:T(8,128)S(1)}, u32[]{:S(2)}, u32[]{:S(2)}) collective-permute-start(f32[2,8,1,256]{3,1,0,2:T(8,128)S(1)} %get-tuple-element.248), channel_id=1, source_target_pairs={{1,0},{2,1},{3,2},{4,3},{5,4},{6,5},{7,6},{8,7},{9,8},{10,9},{11,1... | collective-permute-start | bytes 49160 | tf_op jit(solution)/shard_map/ppermute | solution.py:21
  76.9 5.9 %collective-permute-start.13 = (f32[2,8,1,256]{3,1,0,2:T(8,128)S(1)}, f32[2,8,1,256]{3,1,0,2:T(8,128)S(1)}, u32[]{:S(2)}, u32[]{:S(2)}) collective-permute-start(f32[2,8,1,256]{3,1,0,2:T(8,128)S(1)} %get-tuple-element.243), channel_id=1, source_target_pairs={{0,1},{1,2},{2,3},{3,4},{4,5},{5,6},{6,7},{7,8},{8,9},{9,10},{10,1... | collective-permute-start | bytes 49160 | tf_op jit(solution)/shard_map/ppermute | solution.py:20
  77.0 5.9 %collective-permute-start.12 = (f32[2,8,1,256]{3,1,0,2:T(8,128)S(1)}, f32[2,8,1,256]{3,1,0,2:T(8,128)S(1)}, u32[]{:S(2)}, u32[]{:S(2)}) collective-permute-start(f32[2,8,1,256]{3,1,0,2:T(8,128)S(1)} %get-tuple-element.242), channel_id=1, source_target_pairs={{1,0},{2,1},{3,2},{4,3},{5,4},{6,5},{7,6},{8,7},{9,8},{10,9},{11,1... | collective-permute-start | bytes 49160 | tf_op jit(solution)/shard_map/ppermute | solution.py:21
  83.1 5.9 %collective-permute-start.15 = (f32[2,8,1,256]{3,1,0,2:T(8,128)S(1)}, f32[2,8,1,256]{3,1,0,2:T(8,128)S(1)}, u32[]{:S(2)}, u32[]{:S(2)}) collective-permute-start(f32[2,8,1,256]{3,1,0,2:T(8,128)S(1)} %get-tuple-element.237), channel_id=1, source_target_pairs={{0,1},{1,2},{2,3},{3,4},{4,5},{5,6},{6,7},{7,8},{8,9},{9,10},{10,1... | collective-permute-start | bytes 49160 | tf_op jit(solution)/shard_map/ppermute | solution.py:20
  83.2 5.9 %collective-permute-start.14 = (f32[2,8,1,256]{3,1,0,2:T(8,128)S(1)}, f32[2,8,1,256]{3,1,0,2:T(8,128)S(1)}, u32[]{:S(2)}, u32[]{:S(2)}) collective-permute-start(f32[2,8,1,256]{3,1,0,2:T(8,128)S(1)} %get-tuple-element.236), channel_id=1, source_target_pairs={{1,0},{2,1},{3,2},{4,3},{5,4},{6,5},{7,6},{8,7},{9,8},{10,9},{11,1... | collective-permute-start | bytes 49160 | tf_op jit(solution)/shard_map/ppermute | solution.py:21
  89.4 5.9 %collective-permute-start.17 = (f32[2,8,1,256]{3,1,0,2:T(8,128)S(1)}, f32[2,8,1,256]{3,1,0,2:T(8,128)S(1)}, u32[]{:S(2)}, u32[]{:S(2)}) collective-permute-start(f32[2,8,1,256]{3,1,0,2:T(8,128)S(1)} %get-tuple-element.231), channel_id=1, source_target_pairs={{0,1},{1,2},{2,3},{3,4},{4,5},{5,6},{6,7},{7,8},{8,9},{9,10},{10,1... | collective-permute-start | bytes 49160 | tf_op jit(solution)/shard_map/ppermute | solution.py:20
  89.5 5.9 %collective-permute-start.16 = (f32[2,8,1,256]{3,1,0,2:T(8,128)S(1)}, f32[2,8,1,256]{3,1,0,2:T(8,128)S(1)}, u32[]{:S(2)}, u32[]{:S(2)}) collective-permute-start(f32[2,8,1,256]{3,1,0,2:T(8,128)S(1)} %get-tuple-element.230), channel_id=1, source_target_pairs={{1,0},{2,1},{3,2},{4,3},{5,4},{6,5},{7,6},{8,7},{9,8},{10,9},{11,1... | collective-permute-start | bytes 49160 | tf_op jit(solution)/shard_map/ppermute | solution.py:21
  98.9 5.9 %collective-permute-start.19 = (f32[2,8,1,256]{3,1,0,2:T(8,128)S(1)}, f32[2,8,1,256]{3,1,0,2:T(8,128)S(1)}, u32[]{:S(2)}, u32[]{:S(2)}) collective-permute-start(f32[2,8,1,256]{3,1,0,2:T(8,128)S(1)} %get-tuple-element.225), channel_id=1, source_target_pairs={{0,1},{1,2},{2,3},{3,4},{4,5},{5,6},{6,7},{7,8},{8,9},{9,10},{10,1... | collective-permute-start | bytes 49160 | tf_op jit(solution)/shard_map/ppermute | solution.py:20
  99.0 5.9 %collective-permute-start.18 = (f32[2,8,1,256]{3,1,0,2:T(8,128)S(1)}, f32[2,8,1,256]{3,1,0,2:T(8,128)S(1)}, u32[]{:S(2)}, u32[]{:S(2)}) collective-permute-start(f32[2,8,1,256]{3,1,0,2:T(8,128)S(1)} %get-tuple-element.224), channel_id=1, source_target_pairs={{1,0},{2,1},{3,2},{4,3},{5,4},{6,5},{7,6},{8,7},{9,8},{10,9},{11,1... | collective-permute-start | bytes 49160 | tf_op jit(solution)/shard_map/ppermute | solution.py:21
  105.1 5.9 %collective-permute-start.21 = (f32[2,8,1,256]{3,1,0,2:T(8,128)S(1)}, f32[2,8,1,256]{3,1,0,2:T(8,128)S(1)}, u32[]{:S(2)}, u32[]{:S(2)}) collective-permute-start(f32[2,8,1,256]{3,1,0,2:T(8,128)S(1)} %get-tuple-element.219), channel_id=1, source_target_pairs={{0,1},{1,2},{2,3},{3,4},{4,5},{5,6},{6,7},{7,8},{8,9},{9,10},{10,1... | collective-permute-start | bytes 49160 | tf_op jit(solution)/shard_map/ppermute | solution.py:20
  105.1 5.9 %collective-permute-start.20 = (f32[2,8,1,256]{3,1,0,2:T(8,128)S(1)}, f32[2,8,1,256]{3,1,0,2:T(8,128)S(1)}, u32[]{:S(2)}, u32[]{:S(2)}) collective-permute-start(f32[2,8,1,256]{3,1,0,2:T(8,128)S(1)} %get-tuple-element.218), channel_id=1, source_target_pairs={{1,0},{2,1},{3,2},{4,3},{5,4},{6,5},{7,6},{8,7},{9,8},{10,9},{11,1... | collective-permute-start | bytes 49160 | tf_op jit(solution)/shard_map/ppermute | solution.py:21
  111.3 5.9 %collective-permute-start.23 = (f32[2,8,1,256]{3,1,0,2:T(8,128)S(1)}, f32[2,8,1,256]{3,1,0,2:T(8,128)S(1)}, u32[]{:S(2)}, u32[]{:S(2)}) collective-permute-start(f32[2,8,1,256]{3,1,0,2:T(8,128)S(1)} %get-tuple-element.213), channel_id=1, source_target_pairs={{0,1},{1,2},{2,3},{3,4},{4,5},{5,6},{6,7},{7,8},{8,9},{9,10},{10,1... | collective-permute-start | bytes 49160 | tf_op jit(solution)/shard_map/ppermute | solution.py:20
  111.3 5.9 %collective-permute-start.22 = (f32[2,8,1,256]{3,1,0,2:T(8,128)S(1)}, f32[2,8,1,256]{3,1,0,2:T(8,128)S(1)}, u32[]{:S(2)}, u32[]{:S(2)}) collective-permute-start(f32[2,8,1,256]{3,1,0,2:T(8,128)S(1)} %get-tuple-element.212), channel_id=1, source_target_pairs={{1,0},{2,1},{3,2},{4,3},{5,4},{6,5},{7,6},{8,7},{9,8},{10,9},{11,1... | collective-permute-start | bytes 49160 | tf_op jit(solution)/shard_map/ppermute | solution.py:21
  117.5 5.9 %collective-permute-start.25 = (f32[2,8,1,256]{3,1,0,2:T(8,128)S(1)}, f32[2,8,1,256]{3,1,0,2:T(8,128)S(1)}, u32[]{:S(2)}, u32[]{:S(2)}) collective-permute-start(f32[2,8,1,256]{3,1,0,2:T(8,128)S(1)} %get-tuple-element.207), channel_id=1, source_target_pairs={{0,1},{1,2},{2,3},{3,4},{4,5},{5,6},{6,7},{7,8},{8,9},{9,10},{10,1... | collective-permute-start | bytes 49160 | tf_op jit(solution)/shard_map/ppermute | solution.py:20
  117.6 5.9 %collective-permute-start.24 = (f32[2,8,1,256]{3,1,0,2:T(8,128)S(1)}, f32[2,8,1,256]{3,1,0,2:T(8,128)S(1)}, u32[]{:S(2)}, u32[]{:S(2)}) collective-permute-start(f32[2,8,1,256]{3,1,0,2:T(8,128)S(1)} %get-tuple-element.206), channel_id=1, source_target_pairs={{1,0},{2,1},{3,2},{4,3},{5,4},{6,5},{7,6},{8,7},{9,8},{10,9},{11,1... | collective-permute-start | bytes 49160 | tf_op jit(solution)/shard_map/ppermute | solution.py:21
  123.8 5.9 %collective-permute-start.27 = (f32[2,8,1,256]{3,1,0,2:T(8,128)S(1)}, f32[2,8,1,256]{3,1,0,2:T(8,128)S(1)}, u32[]{:S(2)}, u32[]{:S(2)}) collective-permute-start(f32[2,8,1,256]{3,1,0,2:T(8,128)S(1)} %get-tuple-element.201), channel_id=1, source_target_pairs={{0,1},{1,2},{2,3},{3,4},{4,5},{5,6},{6,7},{7,8},{8,9},{9,10},{10,1... | collective-permute-start | bytes 49160 | tf_op jit(solution)/shard_map/ppermute | solution.py:20
  123.9 5.9 %collective-permute-start.26 = (f32[2,8,1,256]{3,1,0,2:T(8,128)S(1)}, f32[2,8,1,256]{3,1,0,2:T(8,128)S(1)}, u32[]{:S(2)}, u32[]{:S(2)}) collective-permute-start(f32[2,8,1,256]{3,1,0,2:T(8,128)S(1)} %get-tuple-element.200), channel_id=1, source_target_pairs={{1,0},{2,1},{3,2},{4,3},{5,4},{6,5},{7,6},{8,7},{9,8},{10,9},{11,1... | collective-permute-start | bytes 49160 | tf_op jit(solution)/shard_map/ppermute | solution.py:21
  130.1 5.9 %collective-permute-start.29 = (f32[2,8,1,256]{3,1,0,2:T(8,128)S(1)}, f32[2,8,1,256]{3,1,0,2:T(8,128)S(1)}, u32[]{:S(2)}, u32[]{:S(2)}) collective-permute-start(f32[2,8,1,256]{3,1,0,2:T(8,128)S(1)} %get-tuple-element.195), channel_id=1, source_target_pairs={{0,1},{1,2},{2,3},{3,4},{4,5},{5,6},{6,7},{7,8},{8,9},{9,10},{10,1... | collective-permute-start | bytes 49160 | tf_op jit(solution)/shard_map/ppermute | solution.py:20
  130.2 5.9 %collective-permute-start.28 = (f32[2,8,1,256]{3,1,0,2:T(8,128)S(1)}, f32[2,8,1,256]{3,1,0,2:T(8,128)S(1)}, u32[]{:S(2)}, u32[]{:S(2)}) collective-permute-start(f32[2,8,1,256]{3,1,0,2:T(8,128)S(1)} %get-tuple-element.194), channel_id=1, source_target_pairs={{1,0},{2,1},{3,2},{4,3},{5,4},{6,5},{7,6},{8,7},{9,8},{10,9},{11,1... | collective-permute-start | bytes 49160 | tf_op jit(solution)/shard_map/ppermute | solution.py:21
  136.6 5.9 %collective-permute-start.31 = (f32[2,8,1,256]{3,1,0,2:T(8,128)S(1)}, f32[2,8,1,256]{3,1,0,2:T(8,128)S(1)}, u32[]{:S(2)}, u32[]{:S(2)}) collective-permute-start(f32[2,8,1,256]{3,1,0,2:T(8,128)S(1)} %get-tuple-element.189), channel_id=1, source_target_pairs={{0,1},{1,2},{2,3},{3,4},{4,5},{5,6},{6,7},{7,8},{8,9},{9,10},{10,1... | collective-permute-start | bytes 49160 | tf_op jit(solution)/shard_map/ppermute | solution.py:20
  136.6 5.9 %collective-permute-start.30 = (f32[2,8,1,256]{3,1,0,2:T(8,128)S(1)}, f32[2,8,1,256]{3,1,0,2:T(8,128)S(1)}, u32[]{:S(2)}, u32[]{:S(2)}) collective-permute-start(f32[2,8,1,256]{3,1,0,2:T(8,128)S(1)} %get-tuple-element.188), channel_id=1, source_target_pairs={{1,0},{2,1},{3,2},{4,3},{5,4},{6,5},{7,6},{8,7},{9,8},{10,9},{11,1... | collective-permute-start | bytes 49160 | tf_op jit(solution)/shard_map/ppermute | solution.py:21
  143.0 5.9 %collective-permute-start.33 = (f32[2,8,1,256]{3,1,0,2:T(8,128)S(1)}, f32[2,8,1,256]{3,1,0,2:T(8,128)S(1)}, u32[]{:S(2)}, u32[]{:S(2)}) collective-permute-start(f32[2,8,1,256]{3,1,0,2:T(8,128)S(1)} %get-tuple-element.183), channel_id=1, source_target_pairs={{0,1},{1,2},{2,3},{3,4},{4,5},{5,6},{6,7},{7,8},{8,9},{9,10},{10,1... | collective-permute-start | bytes 49160 | tf_op jit(solution)/shard_map/ppermute | solution.py:20
  143.1 5.9 %collective-permute-start.32 = (f32[2,8,1,256]{3,1,0,2:T(8,128)S(1)}, f32[2,8,1,256]{3,1,0,2:T(8,128)S(1)}, u32[]{:S(2)}, u32[]{:S(2)}) collective-permute-start(f32[2,8,1,256]{3,1,0,2:T(8,128)S(1)} %get-tuple-element.182), channel_id=1, source_target_pairs={{1,0},{2,1},{3,2},{4,3},{5,4},{6,5},{7,6},{8,7},{9,8},{10,9},{11,1... | collective-permute-start | bytes 49160 | tf_op jit(solution)/shard_map/ppermute | solution.py:21
  149.6 8.3 %collective-permute-start.35 = (f32[2,8,1,256]{3,1,0,2:T(8,128)S(1)}, f32[2,8,1,256]{3,1,0,2:T(8,128)S(1)}, u32[]{:S(2)}, u32[]{:S(2)}) collective-permute-start(f32[2,8,1,256]{3,1,0,2:T(8,128)S(1)} %get-tuple-element.177), channel_id=1, source_target_pairs={{0,1},{1,2},{2,3},{3,4},{4,5},{5,6},{6,7},{7,8},{8,9},{9,10},{10,1... | collective-permute-start | bytes 49160 | tf_op jit(solution)/shard_map/ppermute | solution.py:20
  149.7 8.3 %collective-permute-start.34 = (f32[2,8,1,256]{3,1,0,2:T(8,128)S(1)}, f32[2,8,1,256]{3,1,0,2:T(8,128)S(1)}, u32[]{:S(2)}, u32[]{:S(2)}) collective-permute-start(f32[2,8,1,256]{3,1,0,2:T(8,128)S(1)} %get-tuple-element.176), channel_id=1, source_target_pairs={{1,0},{2,1},{3,2},{4,3},{5,4},{6,5},{7,6},{8,7},{9,8},{10,9},{11,1... | collective-permute-start | bytes 49160 | tf_op jit(solution)/shard_map/ppermute | solution.py:21
  158.2 5.9 %collective-permute-start.37 = (f32[2,8,1,256]{3,1,0,2:T(8,128)S(1)}, f32[2,8,1,256]{3,1,0,2:T(8,128)S(1)}, u32[]{:S(2)}, u32[]{:S(2)}) collective-permute-start(f32[2,8,1,256]{3,1,0,2:T(8,128)S(1)} %get-tuple-element.171), channel_id=1, source_target_pairs={{0,1},{1,2},{2,3},{3,4},{4,5},{5,6},{6,7},{7,8},{8,9},{9,10},{10,1... | collective-permute-start | bytes 49160 | tf_op jit(solution)/shard_map/ppermute | solution.py:20
  164.4 5.9 %collective-permute-start.39 = (f32[2,8,1,256]{3,1,0,2:T(8,128)S(1)}, f32[2,8,1,256]{3,1,0,2:T(8,128)S(1)}, u32[]{:S(2)}, u32[]{:S(2)}) collective-permute-start(f32[2,8,1,256]{3,1,0,2:T(8,128)S(1)} %get-tuple-element.165), channel_id=1, source_target_pairs={{0,1},{1,2},{2,3},{3,4},{4,5},{5,6},{6,7},{7,8},{8,9},{9,10},{10,1... | collective-permute-start | bytes 49160 | tf_op jit(solution)/shard_map/ppermute | solution.py:20
  164.4 5.9 %collective-permute-start.38 = (f32[2,8,1,256]{3,1,0,2:T(8,128)S(1)}, f32[2,8,1,256]{3,1,0,2:T(8,128)S(1)}, u32[]{:S(2)}, u32[]{:S(2)}) collective-permute-start(f32[2,8,1,256]{3,1,0,2:T(8,128)S(1)} %get-tuple-element.164), channel_id=1, source_target_pairs={{1,0},{2,1},{3,2},{4,3},{5,4},{6,5},{7,6},{8,7},{9,8},{10,9},{11,1... | collective-permute-start | bytes 49160 | tf_op jit(solution)/shard_map/ppermute | solution.py:21
  170.6 5.9 %collective-permute-start.41 = (f32[2,8,1,256]{3,1,0,2:T(8,128)S(1)}, f32[2,8,1,256]{3,1,0,2:T(8,128)S(1)}, u32[]{:S(2)}, u32[]{:S(2)}) collective-permute-start(f32[2,8,1,256]{3,1,0,2:T(8,128)S(1)} %get-tuple-element.159), channel_id=1, source_target_pairs={{0,1},{1,2},{2,3},{3,4},{4,5},{5,6},{6,7},{7,8},{8,9},{9,10},{10,1... | collective-permute-start | bytes 49160 | tf_op jit(solution)/shard_map/ppermute | solution.py:20
  170.7 6.1 %collective-permute-start.40 = (f32[2,8,1,256]{3,1,0,2:T(8,128)S(1)}, f32[2,8,1,256]{3,1,0,2:T(8,128)S(1)}, u32[]{:S(2)}, u32[]{:S(2)}) collective-permute-start(f32[2,8,1,256]{3,1,0,2:T(8,128)S(1)} %get-tuple-element.158), channel_id=1, source_target_pairs={{1,0},{2,1},{3,2},{4,3},{5,4},{6,5},{7,6},{8,7},{9,8},{10,9},{11,1... | collective-permute-start | bytes 49160 | tf_op jit(solution)/shard_map/ppermute | solution.py:21
  177.1 5.9 %collective-permute-start.43 = (f32[2,8,1,256]{3,1,0,2:T(8,128)S(1)}, f32[2,8,1,256]{3,1,0,2:T(8,128)S(1)}, u32[]{:S(2)}, u32[]{:S(2)}) collective-permute-start(f32[2,8,1,256]{3,1,0,2:T(8,128)S(1)} %get-tuple-element.153), channel_id=1, source_target_pairs={{0,1},{1,2},{2,3},{3,4},{4,5},{5,6},{6,7},{7,8},{8,9},{9,10},{10,1... | collective-permute-start | bytes 49160 | tf_op jit(solution)/shard_map/ppermute | solution.py:20
  177.1 5.9 %collective-permute-start.42 = (f32[2,8,1,256]{3,1,0,2:T(8,128)S(1)}, f32[2,8,1,256]{3,1,0,2:T(8,128)S(1)}, u32[]{:S(2)}, u32[]{:S(2)}) collective-permute-start(f32[2,8,1,256]{3,1,0,2:T(8,128)S(1)} %get-tuple-element.152), channel_id=1, source_target_pairs={{1,0},{2,1},{3,2},{4,3},{5,4},{6,5},{7,6},{8,7},{9,8},{10,9},{11,1... | collective-permute-start | bytes 49160 | tf_op jit(solution)/shard_map/ppermute | solution.py:21
  183.4 5.9 %collective-permute-start.45 = (f32[2,8,1,256]{3,1,0,2:T(8,128)S(1)}, f32[2,8,1,256]{3,1,0,2:T(8,128)S(1)}, u32[]{:S(2)}, u32[]{:S(2)}) collective-permute-start(f32[2,8,1,256]{3,1,0,2:T(8,128)S(1)} %get-tuple-element.147), channel_id=1, source_target_pairs={{0,1},{1,2},{2,3},{3,4},{4,5},{5,6},{6,7},{7,8},{8,9},{9,10},{10,1... | collective-permute-start | bytes 49160 | tf_op jit(solution)/shard_map/ppermute | solution.py:20
  183.5 5.9 %collective-permute-start.44 = (f32[2,8,1,256]{3,1,0,2:T(8,128)S(1)}, f32[2,8,1,256]{3,1,0,2:T(8,128)S(1)}, u32[]{:S(2)}, u32[]{:S(2)}) collective-permute-start(f32[2,8,1,256]{3,1,0,2:T(8,128)S(1)} %get-tuple-element.146), channel_id=1, source_target_pairs={{1,0},{2,1},{3,2},{4,3},{5,4},{6,5},{7,6},{8,7},{9,8},{10,9},{11,1... | collective-permute-start | bytes 49160 | tf_op jit(solution)/shard_map/ppermute | solution.py:21
  189.8 5.9 %collective-permute-start.47 = (f32[2,8,1,256]{3,1,0,2:T(8,128)S(1)}, f32[2,8,1,256]{3,1,0,2:T(8,128)S(1)}, u32[]{:S(2)}, u32[]{:S(2)}) collective-permute-start(f32[2,8,1,256]{3,1,0,2:T(8,128)S(1)} %get-tuple-element.141), channel_id=1, source_target_pairs={{0,1},{1,2},{2,3},{3,4},{4,5},{5,6},{6,7},{7,8},{8,9},{9,10},{10,1... | collective-permute-start | bytes 49160 | tf_op jit(solution)/shard_map/ppermute | solution.py:20
  189.9 5.9 %collective-permute-start.46 = (f32[2,8,1,256]{3,1,0,2:T(8,128)S(1)}, f32[2,8,1,256]{3,1,0,2:T(8,128)S(1)}, u32[]{:S(2)}, u32[]{:S(2)}) collective-permute-start(f32[2,8,1,256]{3,1,0,2:T(8,128)S(1)} %get-tuple-element.140), channel_id=1, source_target_pairs={{1,0},{2,1},{3,2},{4,3},{5,4},{6,5},{7,6},{8,7},{9,8},{10,9},{11,1... | collective-permute-start | bytes 49160 | tf_op jit(solution)/shard_map/ppermute | solution.py:21
  196.4 5.9 %collective-permute-start.49 = (f32[2,8,1,256]{3,1,0,2:T(8,128)S(1)}, f32[2,8,1,256]{3,1,0,2:T(8,128)S(1)}, u32[]{:S(2)}, u32[]{:S(2)}) collective-permute-start(f32[2,8,1,256]{3,1,0,2:T(8,128)S(1)} %get-tuple-element.135), channel_id=1, source_target_pairs={{0,1},{1,2},{2,3},{3,4},{4,5},{5,6},{6,7},{7,8},{8,9},{9,10},{10,1... | collective-permute-start | bytes 49160 | tf_op jit(solution)/shard_map/ppermute | solution.py:20
  196.5 5.9 %collective-permute-start.48 = (f32[2,8,1,256]{3,1,0,2:T(8,128)S(1)}, f32[2,8,1,256]{3,1,0,2:T(8,128)S(1)}, u32[]{:S(2)}, u32[]{:S(2)}) collective-permute-start(f32[2,8,1,256]{3,1,0,2:T(8,128)S(1)} %get-tuple-element.134), channel_id=1, source_target_pairs={{1,0},{2,1},{3,2},{4,3},{5,4},{6,5},{7,6},{8,7},{9,8},{10,9},{11,1... | collective-permute-start | bytes 49160 | tf_op jit(solution)/shard_map/ppermute | solution.py:21
  205.6 11.4 %collective-permute-start.51 = (f32[2,8,1,256]{3,1,0,2:T(8,128)}, f32[2,8,1,256]{3,1,0,2:T(8,128)}, u32[]{:S(2)}, u32[]{:S(2)}) collective-permute-start(f32[2,8,1,256]{3,1,0,2:T(8,128)} %get-tuple-element.129), channel_id=1, source_target_pairs={{0,1},{1,2},{2,3},{3,4},{4,5},{5,6},{6,7},{7,8},{8,9},{9,10},{10,1... | collective-permute-start | bytes 49160 | tf_op jit(solution)/shard_map/ppermute | solution.py:20
  205.6 11.4 %collective-permute-start.50 = (f32[2,8,1,256]{3,1,0,2:T(8,128)}, f32[2,8,1,256]{3,1,0,2:T(8,128)}, u32[]{:S(2)}, u32[]{:S(2)}) collective-permute-start(f32[2,8,1,256]{3,1,0,2:T(8,128)} %get-tuple-element.128), channel_id=1, source_target_pairs={{1,0},{2,1},{3,2},{4,3},{5,4},{6,5},{7,6},{8,7},{9,8},{10,9},{11,1... | collective-permute-start | bytes 49160 | tf_op jit(solution)/shard_map/ppermute | solution.py:21
  218.3 5.9 %collective-permute-start.53 = (f32[2,8,1,256]{3,1,0,2:T(8,128)S(1)}, f32[2,8,1,256]{3,1,0,2:T(8,128)S(1)}, u32[]{:S(2)}, u32[]{:S(2)}) collective-permute-start(f32[2,8,1,256]{3,1,0,2:T(8,128)S(1)} %get-tuple-element.123), channel_id=1, source_target_pairs={{0,1},{1,2},{2,3},{3,4},{4,5},{5,6},{6,7},{7,8},{8,9},{9,10},{10,1... | collective-permute-start | bytes 49160 | tf_op jit(solution)/shard_map/ppermute | solution.py:20
  218.4 5.9 %collective-permute-start.52 = (f32[2,8,1,256]{3,1,0,2:T(8,128)S(1)}, f32[2,8,1,256]{3,1,0,2:T(8,128)S(1)}, u32[]{:S(2)}, u32[]{:S(2)}) collective-permute-start(f32[2,8,1,256]{3,1,0,2:T(8,128)S(1)} %get-tuple-element.122), channel_id=1, source_target_pairs={{1,0},{2,1},{3,2},{4,3},{5,4},{6,5},{7,6},{8,7},{9,8},{10,9},{11,1... | collective-permute-start | bytes 49160 | tf_op jit(solution)/shard_map/ppermute | solution.py:21
  224.4 5.9 %collective-permute-start.55 = (f32[2,8,1,256]{3,1,0,2:T(8,128)S(1)}, f32[2,8,1,256]{3,1,0,2:T(8,128)S(1)}, u32[]{:S(2)}, u32[]{:S(2)}) collective-permute-start(f32[2,8,1,256]{3,1,0,2:T(8,128)S(1)} %get-tuple-element.117), channel_id=1, source_target_pairs={{0,1},{1,2},{2,3},{3,4},{4,5},{5,6},{6,7},{7,8},{8,9},{9,10},{10,1... | collective-permute-start | bytes 49160 | tf_op jit(solution)/shard_map/ppermute | solution.py:20
  224.5 5.9 %collective-permute-start.54 = (f32[2,8,1,256]{3,1,0,2:T(8,128)S(1)}, f32[2,8,1,256]{3,1,0,2:T(8,128)S(1)}, u32[]{:S(2)}, u32[]{:S(2)}) collective-permute-start(f32[2,8,1,256]{3,1,0,2:T(8,128)S(1)} %get-tuple-element.116), channel_id=1, source_target_pairs={{1,0},{2,1},{3,2},{4,3},{5,4},{6,5},{7,6},{8,7},{9,8},{10,9},{11,1... | collective-permute-start | bytes 49160 | tf_op jit(solution)/shard_map/ppermute | solution.py:21
  230.7 5.9 %collective-permute-start.57 = (f32[2,8,1,256]{3,1,0,2:T(8,128)S(1)}, f32[2,8,1,256]{3,1,0,2:T(8,128)S(1)}, u32[]{:S(2)}, u32[]{:S(2)}) collective-permute-start(f32[2,8,1,256]{3,1,0,2:T(8,128)S(1)} %get-tuple-element.111), channel_id=1, source_target_pairs={{0,1},{1,2},{2,3},{3,4},{4,5},{5,6},{6,7},{7,8},{8,9},{9,10},{10,1... | collective-permute-start | bytes 49160 | tf_op jit(solution)/shard_map/ppermute | solution.py:20
  230.7 5.9 %collective-permute-start.56 = (f32[2,8,1,256]{3,1,0,2:T(8,128)S(1)}, f32[2,8,1,256]{3,1,0,2:T(8,128)S(1)}, u32[]{:S(2)}, u32[]{:S(2)}) collective-permute-start(f32[2,8,1,256]{3,1,0,2:T(8,128)S(1)} %get-tuple-element.110), channel_id=1, source_target_pairs={{1,0},{2,1},{3,2},{4,3},{5,4},{6,5},{7,6},{8,7},{9,8},{10,9},{11,1... | collective-permute-start | bytes 49160 | tf_op jit(solution)/shard_map/ppermute | solution.py:21
  237.0 5.9 %collective-permute-start.59 = (f32[2,8,1,256]{3,1,0,2:T(8,128)S(1)}, f32[2,8,1,256]{3,1,0,2:T(8,128)S(1)}, u32[]{:S(2)}, u32[]{:S(2)}) collective-permute-start(f32[2,8,1,256]{3,1,0,2:T(8,128)S(1)} %get-tuple-element.105), channel_id=1, source_target_pairs={{0,1},{1,2},{2,3},{3,4},{4,5},{5,6},{6,7},{7,8},{8,9},{9,10},{10,1... | collective-permute-start | bytes 49160 | tf_op jit(solution)/shard_map/ppermute | solution.py:20
  237.0 5.9 %collective-permute-start.58 = (f32[2,8,1,256]{3,1,0,2:T(8,128)S(1)}, f32[2,8,1,256]{3,1,0,2:T(8,128)S(1)}, u32[]{:S(2)}, u32[]{:S(2)}) collective-permute-start(f32[2,8,1,256]{3,1,0,2:T(8,128)S(1)} %get-tuple-element.104), channel_id=1, source_target_pairs={{1,0},{2,1},{3,2},{4,3},{5,4},{6,5},{7,6},{8,7},{9,8},{10,9},{11,1... | collective-permute-start | bytes 49160 | tf_op jit(solution)/shard_map/ppermute | solution.py:21
  243.2 5.9 %collective-permute-start.61 = (f32[2,8,1,256]{3,1,0,2:T(8,128)S(1)}, f32[2,8,1,256]{3,1,0,2:T(8,128)S(1)}, u32[]{:S(2)}, u32[]{:S(2)}) collective-permute-start(f32[2,8,1,256]{3,1,0,2:T(8,128)S(1)} %get-tuple-element.99), channel_id=1, source_target_pairs={{0,1},{1,2},{2,3},{3,4},{4,5},{5,6},{6,7},{7,8},{8,9},{9,10},{10,1... | collective-permute-start | bytes 49160 | tf_op jit(solution)/shard_map/ppermute | solution.py:20
  243.2 5.9 %collective-permute-start.60 = (f32[2,8,1,256]{3,1,0,2:T(8,128)S(1)}, f32[2,8,1,256]{3,1,0,2:T(8,128)S(1)}, u32[]{:S(2)}, u32[]{:S(2)}) collective-permute-start(f32[2,8,1,256]{3,1,0,2:T(8,128)S(1)} %get-tuple-element.98), channel_id=1, source_target_pairs={{1,0},{2,1},{3,2},{4,3},{5,4},{6,5},{7,6},{8,7},{9,8},{10,9},{11,1... | collective-permute-start | bytes 49160 | tf_op jit(solution)/shard_map/ppermute | solution.py:21
  249.4 5.9 %collective-permute-start.63 = (f32[2,8,1,256]{3,1,0,2:T(8,128)S(1)}, f32[2,8,1,256]{3,1,0,2:T(8,128)S(1)}, u32[]{:S(2)}, u32[]{:S(2)}) collective-permute-start(f32[2,8,1,256]{3,1,0,2:T(8,128)S(1)} %get-tuple-element.93), channel_id=1, source_target_pairs={{0,1},{1,2},{2,3},{3,4},{4,5},{5,6},{6,7},{7,8},{8,9},{9,10},{10,1... | collective-permute-start | bytes 49160 | tf_op jit(solution)/shard_map/ppermute | solution.py:20
  249.5 5.9 %collective-permute-start.62 = (f32[2,8,1,256]{3,1,0,2:T(8,128)S(1)}, f32[2,8,1,256]{3,1,0,2:T(8,128)S(1)}, u32[]{:S(2)}, u32[]{:S(2)}) collective-permute-start(f32[2,8,1,256]{3,1,0,2:T(8,128)S(1)} %get-tuple-element.92), channel_id=1, source_target_pairs={{1,0},{2,1},{3,2},{4,3},{5,4},{6,5},{7,6},{8,7},{9,8},{10,9},{11,1... | collective-permute-start | bytes 49160 | tf_op jit(solution)/shard_map/ppermute | solution.py:21
  256.1 5.9 %collective-permute-start.65 = (f32[2,8,1,256]{3,1,0,2:T(8,128)S(1)}, f32[2,8,1,256]{3,1,0,2:T(8,128)S(1)}, u32[]{:S(2)}, u32[]{:S(2)}) collective-permute-start(f32[2,8,1,256]{3,1,0,2:T(8,128)S(1)} %get-tuple-element.91), channel_id=1, source_target_pairs={{0,1},{1,2},{2,3},{3,4},{4,5},{5,6},{6,7},{7,8},{8,9},{9,10},{10,1... | collective-permute-start | bytes 49160 | tf_op jit(solution)/shard_map/ppermute | solution.py:20
  256.1 5.9 %collective-permute-start.64 = (f32[2,8,1,256]{3,1,0,2:T(8,128)S(1)}, f32[2,8,1,256]{3,1,0,2:T(8,128)S(1)}, u32[]{:S(2)}, u32[]{:S(2)}) collective-permute-start(f32[2,8,1,256]{3,1,0,2:T(8,128)S(1)} %get-tuple-element.90), channel_id=1, source_target_pairs={{1,0},{2,1},{3,2},{4,3},{5,4},{6,5},{7,6},{8,7},{9,8},{10,9},{11,1... | collective-permute-start | bytes 49160 | tf_op jit(solution)/shard_map/ppermute | solution.py:21
  (138 other events, 2332.6 us)
where the time goes:
time: 289 us; the launch traced here: 287 us
  starting transfers between devices  150 us (52%)
  waiting for transfers between devices  41.2 us (14%)
  other arithmetic  33.1 us (11%)
  between operations  29 us (10%)
  blocking collectives  19.4 us (7%)
  local copies, waits for them, and re-layouts  14.5 us (5%)
    ppermute x33, starting transfers between devices, padded(): after = lax.ppermute(first, axis, down)  149 us
    ppermute x33, waiting for transfers between devices, padded(): before = lax.ppermute(last, axis, up)  39.2 us
    all_gather x1, blocking collectives, per_device(): whole = lax.all_gather(outgoing, 'sector', axis=2, tiled=True)  19.4 us
    add x4, other arithmetic, per_device(): rhs = sig * state + waveform[step] * source  14.7 us
  transfers between devices with their start and end apart: 66, of which 55 were waited for; matrix products, arithmetic and copies ran while one was open for 4% of the time, Pallas kernels for 0%

commit v1 on v0

v1 whole, which is shorter than its diff:
```python
import functools

import jax
import jax.numpy as jnp
from jax import lax
from jax.experimental import pallas as pl
from jax.experimental.pallas import tpu as pltpu
from jax.sharding import PartitionSpec as P

DEG = 8
THETA = 1.05
DELTA = 0.95
CHUNK = 4


def rates(count):
    rho = DELTA / THETA
    first = []
    second = []
    for step in range(count):
        fresh = 1.0 / (2.0 * THETA / DELTA - rho)
        first.append(fresh * rho)
        second.append(2.0 * fresh / DELTA)
        rho = fresh
    return (first, second)


def chunks(start, stop):
    return [(at, min(CHUNK, stop - at)) for at in range(start, stop, CHUNK)]


def kernel(
    count, cells, steps, radial, axial, mats,
    waveform, degrees, offsets, conduct, reluct, robin, packed,
    field_out, next_out,
    got, nu, sig, aplus, aminus, rplus, rminus, zplus, zminus, own, dsrc, dtop,
    state, resid, direct, staged,
    send_mat, recv_mat, send_rest, recv_rest, send_halo, recv_halo,
    send_trace, recv_trace, send_last, recv_last, *whole,
):
    chips = count // 2
    wide = 2 * cells
    ext = 3 * wide
    group = lax.axis_index("groups")
    place = lax.axis_index("sector")
    chip = lax.div(place, 2)
    core = lax.rem(place, 2)
    other = 1 - core

    def device(to_chip, to_core):
        return {"groups": group, "sector": 2 * to_chip + to_core}

    def away(distance):
        return lax.rem(chip + distance + chips, chips)

    def copy(src, dst, send, recv, target):
        return pltpu.make_async_remote_copy(
            src_ref=src, dst_ref=dst, send_sem=send, recv_sem=recv,
            device_id=target, device_id_type=pl.DeviceIdType.MESH,
        )

    barrier = pltpu.get_barrier_semaphore()
    partners = [device(away(d), core) for d in range(1, chips)]
    partners += [device(away(d), other) for d in (-1, 0, 1)]
    for target in partners:
        pl.semaphore_signal(barrier, inc=1, device_id=target, device_id_type=pl.DeviceIdType.MESH)
    got[1, core] = packed[core]
    pl.semaphore_wait(barrier, len(partners))

    tiles = packed.shape[1]
    moves = []
    for part, send, recv in (((0, cells), send_mat, recv_mat), ((cells, tiles - cells), send_rest, recv_rest)):
        first, size = part
        line = []
        for d, flip in ((-1, 0), (1, 0), (-1, 1), (1, 1), (0, 1)):
            to_core = other if flip else core
            line.append(copy(
                packed.at[to_core, pl.ds(first, size)],
                got.at[1 - d, core, pl.ds(first, size)],
                send.at[1 + d, flip], recv.at[1 - d, core],
                device(away(d), to_core),
            ))
        for move in line:
            move.start()
        moves.append(line)

    def arrive(recv, first, size):
        for d, flip in ((-1, 0), (1, 0), (-1, 1), (1, 1), (0, 1)):
            from_core = other if flip else core
            copy(
                packed.at[core, pl.ds(first, size)],
                got.at[1 + d, from_core, pl.ds(first, size)],
                send_mat.at[0, 0], recv.at[1 + d, from_core],
                device(away(d), from_core),
            ).wait_recv()

    def block(cell):
        return cell // wide, (cell // cells) % 2, cell % cells

    arrive(recv_mat, 0, cells)
    rob = robin[core]
    for a in range(0, ext, cells):
        i, k, _ = block(a)
        kind = got[i, k, 0:cells]
        nu_new = jnp.zeros(kind.shape, jnp.float32)
        sig_new = jnp.zeros(kind.shape, jnp.float32)
        for index in range(mats):
            hit = kind == float(index)
            nu_new = nu_new + jnp.where(hit, reluct[index], 0.0)
            sig_new = sig_new + jnp.where(hit, conduct[index], 0.0)
        nu[a : a + cells] = nu_new
        sig[a : a + cells] = sig_new
    for a, n in chunks(1, ext - 1):
        shape = (n, radial, axial)
        rpos = lax.broadcasted_iota(jnp.int32, shape, 1)
        zpos = lax.broadcasted_iota(jnp.int32, shape, 2)
        here = nu[a : a + n]
        cond = sig[a : a + n]
        kap = 0.5 * (here + nu[a + 1 : a + n + 1])
        kam = 0.5 * (here + nu[a - 1 : a + n - 1])
        low, top = rpos == 0, rpos == radial - 1
        front, back = zpos == 0, zpos == axial - 1
        krp = jnp.where(top, 0.0, 0.5 * (here + pltpu.roll(here, radial - 1, 1)))
        krm = jnp.where(low, 0.0, 0.5 * (here + pltpu.roll(here, 1, 1)))
        kzp = jnp.where(back, 0.0, 0.5 * (here + pltpu.roll(here, axial - 1, 2)))
        kzm = jnp.where(front, 0.0, 0.5 * (here + pltpu.roll(here, 1, 2)))
        border = jnp.where(low, here, 0.0) + jnp.where(front, here, 0.0)
        border = border + jnp.where(back, here, 0.0) + jnp.where(top, rob, 0.0)
        diag = cond + kap + kam + krp + krm + kzp + kzm + border
        dinv = 1.0 / diag
        aplus[a : a + n] = dinv * kap
        aminus[a : a + n] = dinv * kam
        rplus[a : a + n] = dinv * krp
        rminus[a : a + n] = dinv * krm
        zplus[a : a + n] = dinv * kzp
        zminus[a : a + n] = dinv * kzm
        own[a : a + n] = dinv * cond - 1.0
        dtop[a : a + n] = jnp.where(top, dinv, 0.0)
        dsrc[a : a + n] = dinv
    arrive(recv_rest, cells, tiles - cells)
    for a in range(0, ext, cells):
        i, k, _ = block(a)
        state[0, a : a + cells] = got[i, k, cells : 2 * cells]
    for a, n in chunks(1, ext - 1):
        for cell in range(a, a + n):
            i, k, j = block(cell)
            dsrc[cell] = dsrc[cell] * got[i, k, 2 * cells + j]

    def given(cell, step):
        i, k, j = block(cell)
        row = j * steps + step
        return got[i, k, 3 * cells + row // radial, row % radial : row % radial + 1, :]

    def beside(src, a, n):
        mid = src[a : a + n]
        total = aplus[a : a + n] * src[a + 1 : a + n + 1]
        total = total + aminus[a : a + n] * src[a - 1 : a + n - 1]
        total = total + rplus[a : a + n] * pltpu.roll(mid, radial - 1, 1)
        total = total + rminus[a : a + n] * pltpu.roll(mid, 1, 1)
        total = total + zplus[a : a + n] * pltpu.roll(mid, axial - 1, 2)
        total = total + zminus[a : a + n] * pltpu.roll(mid, 1, 2)
        return mid, total

    first, second = rates(DEG)
    halo_moves = []
    trace_moves = []
    for step in range(steps):
        if step > 0:
            for line in halo_moves[-1]:
                line.wait_recv()
        here = state.at[step]
        wave = waveform[step]
        degree = degrees[step]
        for a, n in chunks(1, ext - 1):
            mid, total = beside(here, a, n)
            extra = jnp.stack([jnp.broadcast_to(given(cell, step), (radial, axial)) for cell in range(a, a + n)])
            fresh = total + own[a : a + n] * mid + wave * dsrc[a : a + n]
            fresh = fresh + dtop[a : a + n] * extra
            resid[a : a + n] = fresh
            direct[0, a : a + n] = fresh * (1.0 / THETA)
        for sweep in range(DEG):
            active = (sweep < degree).astype(jnp.float32)
            old = direct.at[sweep % 2]
            new = direct.at[(sweep + 1) % 2]
            base = here if sweep == 0 else state.at[step + 1]
            for a, n in chunks(wide, 2 * wide):
                state[step + 1, a : a + n] = base[a : a + n] + active * old[a : a + n]
            if sweep == DEG - 1:
                break
            for a, n in chunks(2 + sweep, ext - 2 - sweep):
                mid, total = beside(old, a, n)
                fresh = resid[a : a + n] - mid + total
                resid[a : a + n] = fresh
                new[a : a + n] = first[sweep] * mid + second[sweep] * fresh
        after = state.at[step + 1]
        if step < steps - 1:
            line = [
                copy(
                    after.at[pl.ds(wide, wide)], after.at[pl.ds((1 - d) * wide, wide)],
                    send_halo.at[step, (d + 1) // 2], recv_halo.at[step, (d + 1) // 2],
                    device(away(d), core),
                )
                for d in (-1, 1)
            ]
            for move in line:
                move.start()
            halo_moves.append(line)
        for cell in range(wide):
            trace = 2.0 * rob * after[wide + cell, radial - 1 : radial, :] - given(wide + cell, step)
            whole[step][chip, cell // cells, cell % cells : cell % cells + 1, :] = trace
        for d in range(1, chips):
            move = copy(
                whole[step].at[chip], whole[step].at[chip],
                send_trace.at[step, d], recv_trace.at[step, d], device(away(d), core),
            )
            move.start()
            trace_moves.append(move)

    last = state.at[steps]
    swap = copy(
        last.at[pl.ds(wide + cells * other, cells)], field_out.at[core],
        send_last.at[0], recv_last.at[0], device(chip, other),
    )
    swap.start()
    field_out[core] = last[pl.ds(wide + cells * core, cells)]
    sign = 2 * core - 1
    for step in range(steps):
        for d in range(1, chips):
            trace_moves[step * (chips - 1) + d - 1].wait_recv()
        shift = sign * offsets[step] + count
        near = lax.rem(place + shift, count)
        far = lax.rem(2 * chip + other + shift, count)
        next_out[other, step] = whole[step][lax.div(near, 2), lax.rem(near, 2)]
        staged[step] = whole[step][lax.div(far, 2), lax.rem(far, 2)]
    swap_next = copy(
        staged, next_out.at[other], send_last.at[1], recv_last.at[1], device(chip, other),
    )
    swap_next.start()
    for line in moves:
        for move in line:
            move.wait_send()
    for line in halo_moves:
        for move in line:
            move.wait_send()
    for move in trace_moves:
        move.wait_send()
    swap.wait()
    swap_next.wait()


def per_device(
    count, field, source, materials, incoming, waveform, degrees, offsets, conduct, reluct, robin
):
    regions, radial, cells, axial = field.shape
    steps = incoming.shape[1]
    chips = count // 2
    turned = [
        jnp.transpose(v, (0, 2, 1, 3)) for v in (materials.astype(jnp.float32), field, source)
    ]
    given = jnp.transpose(incoming, (0, 2, 1, 3)).reshape(regions, -1, radial, axial)
    packed = jnp.concatenate(turned + [given], axis=1)
    tiles = packed.shape[1]
    ext = 6 * cells
    vmem = pl.BlockSpec(memory_space=pltpu.VMEM)
    smem = pl.BlockSpec(memory_space=pltpu.SMEM)

    def area(*lead):
        return pltpu.VMEM((*lead, radial, axial), jnp.float32)

    dma = pltpu.SemaphoreType.DMA
    field_end, next_incoming = pl.pallas_call(
        functools.partial(kernel, count, cells, steps, radial, axial, conduct.shape[0]),
        out_shape=(
            jax.ShapeDtypeStruct((regions, cells, radial, axial), jnp.float32),
            jax.ShapeDtypeStruct((regions, steps, cells, axial), jnp.float32),
        ),
        in_specs=[smem] * 6 + [vmem],
        out_specs=(vmem, vmem),
        scratch_shapes=[
            area(3, 2, tiles),
            *[area(ext) for _ in range(11)],
            area(steps + 1, ext),
            area(ext),
            area(2, ext),
            pltpu.VMEM((steps, cells, axial), jnp.float32),
            dma((3, 2)),
            dma((3, 2)),
            dma((3, 2)),
            dma((3, 2)),
            dma((steps, 2)),
            dma((steps, 2)),
            dma((steps, chips)),
            dma((steps, chips)),
            dma((2,)),
            dma((2,)),
            *[pltpu.VMEM((chips, 2, cells, axial), jnp.float32) for _ in range(steps)],
        ],
        compiler_params=pltpu.CompilerParams(
            collective_id=0, has_side_effects=True, vmem_limit_bytes=32 * 1024 * 1024
        ),
        name="window",
    )(waveform, degrees, offsets, conduct, reluct, robin, packed)
    return (jnp.transpose(field_end, (0, 2, 1, 3)), next_incoming)


def solution(mesh):
    return jax.shard_map(
        functools.partial(per_device, mesh.shape["sector"]),
        mesh=mesh,
        in_specs=(
            P("groups", None, "sector", None),
            P("groups", None, "sector", None),
            P("groups", None, "sector", None),
            P("groups", None, "sector", None),
            P("groups"),
            P("groups"),
            P("groups"),
            P(),
            P(),
            P(),
        ),
        out_specs=(P("groups", None, "sector", None), P("groups", None, "sector", None)),
        check_vma=False,
    )
```

time: 289 us -> 46.4 us (0.16)
  starting transfers between devices: 150 us -> 0 us
  Pallas kernels: 0 us -> 41.7 us
  waiting for transfers between devices: 41.2 us -> 0 us
  other arithmetic: 33.1 us -> 0.03 us
  between operations: 29 us -> 0.74 us
  blocking collectives: 19.4 us -> 0 us
  local copies, waits for them, and re-layouts: 14.5 us -> 3.62 us
    ppermute x66 -> x0, starting transfers between devices: 150 us -> none  [the longest x33 149 us: padded(): after = lax.ppermute(first, axis, down)]
    pallas_call x0 -> x1, Pallas kernels: none -> 41.7 us  [per_device(): pl.pallas_call(functools.partial(kernel, count, cells, steps, radial, axi...]
    ppermute x66 -> x0, waiting for transfers between devices: 41.2 us -> none  [the longest x33 39.2 us: padded(): before = lax.ppermute(last, axis, up)]
    add x35 -> x0, other arithmetic: 24.4 us -> none  [the longest x4 14.7 us: per_device(): rhs = sig * state + waveform[step] * source]
    all_gather x1 -> x0, blocking collectives: 19.4 us -> none  [per_device(): whole = lax.all_gather(outgoing, 'sector', axis=2, tiled=True)]
    slice x103 -> x0, local copies, waits for them, and re-layouts: 9.89 us -> none  [the longest x32 3.17 us: operate(): up_z = jnp.concatenate([x_c[..., 1:], zero_z], 3)]
    another operation x5 -> x0, other arithmetic: 5.53 us -> none  [the longest x1 4.85 us: per_device(): both_ext = padded(jnp.stack([nu, sig]), (('sector', 3),), depth)]
  transfers between devices with their start and end apart: 66 -> 0, of which waited for: 55 -> 0; matrix products, arithmetic and copies ran while one was open for 4% -> 0% of each run, Pallas kernels for 0% -> 0%
where the time goes in v1:
time: 46.4 us; the launch traced here: 46.1 us
  Pallas kernels  41.7 us (90%)
  local copies, waits for them, and re-layouts  3.62 us (8%)
  between operations  0.74 us (2%)
    pallas_call x1, Pallas kernels, per_device(): pl.pallas_call(functools.partial(kernel, count, cells, steps, radial, axi...  41.7 us
    unnamed x20, local copies, waits for them, and re-layouts  2.78 us

profile of v1, /device:TPU:0, one launch (start us, length us, event | category | flops | bytes accessed | tf_op | source)
XLA Modules:
  0.0 46.1 jit_solution(11578551200905962835)
XLA Ops:
  0.6 0.0 copy-start.6
  0.6 0.8 %copy.15 = f32[2,4,4,256]{3,2,1,0:T(4,128)S(1)} copy(f32[2,4,4,256]{3,1,2,0:T(4,128)} %bitcast.9) | data formatting | bytes 65536 | tf_op jit(solution)/shard_map/transpose | solution.py:260
  1.5 0.0 copy-done.6
  1.5 0.0 copy-start.7
  1.5 0.0 copy-start.8
  1.5 0.8 %copy-done.7 = f32[2,8,4,256]{3,2,1,0:T(4,128)S(1)} copy-done((f32[2,8,4,256]{3,2,1,0:T(4,128)S(1)}, f32[2,8,4,256]{3,2,1,0:T(4,128)}, u32[]{:S(2)}) %copy-start.7) | copy-done | bytes 65560
  2.3 0.0 copy-done.8
  2.4 0.0 copy-start
  2.4 0.0 copy-start.1
  2.4 0.0 copy-start.2
  2.4 0.0 copy-start.3
  2.4 0.0 copy-start.4
  2.4 0.0 copy-start.5
  2.5 0.6 %copy-done = f32[4]{0:T(128)S(1)} copy-done((f32[4]{0:T(128)S(1)}, f32[4]{0:T(128)}, u32[]{:S(2)}) %copy-start) | copy-done | bytes 40
  3.0 0.0 copy-done.1
  3.1 0.0 copy-done.2
  3.1 0.0 copy-done.3
  3.1 0.0 copy-done.4
  3.1 0.0 copy-done.5
  3.1 41.7 %window.1 = (f32[2,4,8,256]{3,2,1,0:T(8,128)S(1)}, f32[2,4,4,256]{3,2,1,0:T(4,128)S(1)}) custom-call(f32[4]{0:T(128)S(1)} %copy-done, s32[4]{0:T(128)S(1)} %copy-done.1, s32[4]{0:T(128)S(1)} %copy-done.2, f32[4]{0:T(128)S(1)} %copy-done.3, f32[4]{0:T(128)S(1)} %copy-done.4, f32[2]{0:T(128)S(1)} %copy-done.5, f32[2,14,8,256]{3,2,1,0:T(8,128)S(1)} %pad_maximum_fusion.packed), custom_call_target="tpu_custom_call" | custom-call | tf_op jit(solution)/shard_map/window/pallas_call | solution.py:271
  44.9 0.7 %copy.16 = f32[2,8,4,256]{3,2,1,0:T(4,128)} copy(f32[2,8,4,256]{3,1,2,0:T(8,128)S(1)} %bitcast.8) | data formatting | bytes 131072
  45.5 0.6 %copy.23 = f32[2,4,4,256]{3,2,1,0:T(4,128)} copy(f32[2,4,4,256]{3,2,1,0:T(4,128)S(1)} %get-tuple-element.13) | data formatting | bytes 65536
  (4 shorter events, 0.1 us)
Async XLA Ops:
  0.6 0.8 %copy-start.6 = (s32[2,8,4,256]{3,2,1,0:T(4,128)S(1)}, s32[2,8,4,256]{3,2,1,0:T(4,128)}, u32[]{:S(2)}) copy-start(s32[2,8,4,256]{3,2,1,0:T(4,128)} %param.12) | copy-start | bytes 196612
  1.5 0.8 %copy-start.7 = (f32[2,8,4,256]{3,2,1,0:T(4,128)S(1)}, f32[2,8,4,256]{3,2,1,0:T(4,128)}, u32[]{:S(2)}) copy-start(f32[2,8,4,256]{3,2,1,0:T(4,128)} %param.11) | copy-start | bytes 196612
  1.5 0.9 %copy-start.8 = (f32[2,8,4,256]{3,2,1,0:T(4,128)S(1)}, f32[2,8,4,256]{3,2,1,0:T(4,128)}, u32[]{:S(2)}) copy-start(f32[2,8,4,256]{3,2,1,0:T(4,128)} %param.10) | copy-start | bytes 196612
  2.4 0.7 %copy-start = (f32[4]{0:T(128)S(1)}, f32[4]{0:T(128)}, u32[]{:S(2)}) copy-start(f32[4]{0:T(128)} %waveform.1) | copy-start | bytes 52
  2.4 0.7 %copy-start.1 = (s32[4]{0:T(128)S(1)}, s32[4]{0:T(128)}, u32[]{:S(2)}) copy-start(s32[4]{0:T(128)} %degrees.1) | copy-start | bytes 52
  2.4 0.7 %copy-start.2 = (s32[4]{0:T(128)S(1)}, s32[4]{0:T(128)}, u32[]{:S(2)}) copy-start(s32[4]{0:T(128)} %offsets.1) | copy-start | bytes 52
  2.4 0.7 %copy-start.3 = (f32[4]{0:T(128)S(1)}, f32[4]{0:T(128)}, u32[]{:S(2)}) copy-start(f32[4]{0:T(128)} %conduct.1) | copy-start | bytes 52
  2.4 0.7 %copy-start.4 = (f32[4]{0:T(128)S(1)}, f32[4]{0:T(128)}, u32[]{:S(2)}) copy-start(f32[4]{0:T(128)} %reluct.1) | copy-start | bytes 52
  2.4 0.7 %copy-start.5 = (f32[2]{0:T(128)S(1)}, f32[2]{0:T(128)}, u32[]{:S(2)}) copy-start(f32[2]{0:T(128)} %robin.1) | copy-start | bytes 28

commit v2 on v1

--- a/solution.py
+++ b/solution.py
@@ -43,12 +43,20 @@
     ext = 3 * wide
     group = lax.axis_index("groups")
     place = lax.axis_index("sector")
-    chip = lax.div(place, 2)
-    core = lax.rem(place, 2)
+    half = lax.rem(place, 2)
+    home = lax.div(place, 2)
+    chip = 2 * lax.div(place, 4) + half
+    core = lax.rem(home, 2)
     other = 1 - core
 
     def device(to_chip, to_core):
-        return {"groups": group, "sector": 2 * to_chip + to_core}
+        return at(sector_of(to_chip, to_core))
+
+    def sector_of(to_chip, to_core):
+        return 4 * lax.div(to_chip, 2) + 2 * to_core + lax.rem(to_chip, 2)
+
+    def at(sector):
+        return {"groups": group, "sector": sector}
 
     def away(distance):
         return lax.rem(chip + distance + chips, chips)
@@ -60,44 +68,55 @@
         )
 
     barrier = pltpu.get_barrier_semaphore()
-    partners = [device(away(d), core) for d in range(1, chips)]
-    partners += [device(away(d), other) for d in (-1, 0, 1)]
+    partners = [at(lax.rem(place + d, count)) for d in range(1, count)]
     for target in partners:
         pl.semaphore_signal(barrier, inc=1, device_id=target, device_id_type=pl.DeviceIdType.MESH)
-    got[1, core] = packed[core]
+    got[1 + home - chip, half] = packed[core]
     pl.semaphore_wait(barrier, len(partners))
 
     tiles = packed.shape[1]
-    moves = []
-    for part, send, recv in (((0, cells), send_mat, recv_mat), ((cells, tiles - cells), send_rest, recv_rest)):
-        first, size = part
-        line = []
-        for d, flip in ((-1, 0), (1, 0), (-1, 1), (1, 1), (0, 1)):
-            to_core = other if flip else core
-            line.append(copy(
-                packed.at[to_core, pl.ds(first, size)],
-                got.at[1 - d, core, pl.ds(first, size)],
-                send.at[1 + d, flip], recv.at[1 - d, core],
-                device(away(d), to_core),
-            ))
-        for move in line:
-            move.start()
-        moves.append(line)
-
-    def arrive(recv, first, size):
-        for d, flip in ((-1, 0), (1, 0), (-1, 1), (1, 1), (0, 1)):
-            from_core = other if flip else core
-            copy(
-                packed.at[core, pl.ds(first, size)],
-                got.at[1 + d, from_core, pl.ds(first, size)],
-                send_mat.at[0, 0], recv.at[1 + d, from_core],
-                device(away(d), from_core),
-            ).wait_recv()
+    parts = ((0, cells, send_mat, recv_mat), (cells, tiles - cells, send_rest, recv_rest))
+
+    def ship(part, begin):
+        first, size, send, recv = part
+        for d in (-1, 1, 0):
+            block_to = lax.rem(home + d + chips, chips)
+            for region in (0, 1):
+                target = sector_of(block_to, region)
+
+                @pl.when(target != place)
+                def _():
+                    move = copy(
+                        packed.at[region, pl.ds(first, size)],
+                        got.at[1 - d, half, pl.ds(first, size)],
+                        send.at[1 + d, region], recv.at[1 - d, half], at(target),
+                    )
+                    if begin:
+                        move.start()
+                    else:
+                        move.wait_send()
+
+    for part in parts:
+        ship(part, True)
+
+    def arrive(part):
+        first, size, send, recv = part
+        for d in (-1, 1, 0):
+            for k in (0, 1):
+                source = 2 * away(d) + k
+
+                @pl.when(source != place)
+                def _():
+                    copy(
+                        packed.at[0, pl.ds(first, size)],
+                        got.at[1 + d, k, pl.ds(first, size)],
+                        send.at[0, 0], recv.at[1 + d, k], at(source),
+                    ).wait_recv()
 
     def block(cell):
         return cell // wide, (cell // cells) % 2, cell % cells
 
-    arrive(recv_mat, 0, cells)
+    arrive(parts[0])
     rob = robin[core]
     for a in range(0, ext, cells):
         i, k, _ = block(a)
@@ -137,7 +156,7 @@
         own[a : a + n] = dinv * cond - 1.0
         dtop[a : a + n] = jnp.where(top, dinv, 0.0)
         dsrc[a : a + n] = dinv
-    arrive(recv_rest, cells, tiles - cells)
+    arrive(parts[1])
     for a in range(0, ext, cells):
         i, k, _ = block(a)
         state[0, a : a + cells] = got[i, k, cells : 2 * cells]
@@ -217,35 +236,64 @@
             trace_moves.append(move)
 
     last = state.at[steps]
-    swap = copy(
-        last.at[pl.ds(wide + cells * other, cells)], field_out.at[core],
-        send_last.at[0], recv_last.at[0], device(chip, other),
-    )
-    swap.start()
-    field_out[core] = last[pl.ds(wide + cells * core, cells)]
+
+    def hand(kind, k, begin):
+        target = 2 * chip + k
+
+        @pl.when(target != place)
+        def _():
+            move = copy(
+                last.at[pl.ds(wide + cells * k, cells)] if kind == 0 else staged.at[k],
+                field_out.at[core] if kind == 0 else next_out.at[other],
+                send_last.at[kind, k], recv_last.at[kind, core], at(target),
+            )
+            if begin:
+                move.start()
+            else:
+                move.wait_send()
+
+        if begin:
+            @pl.when(target == place)
+            def _():
+                if kind == 0:
+                    field_out[core] = last[wide + cells * k : wide + cells * k + cells]
+                else:
+                    next_out[other] = staged[k]
+
+    def take(kind, region):
+        source = sector_of(home, region)
+
+        @pl.when(source != place)
+        def _():
+            copy(
+                last.at[pl.ds(wide, cells)] if kind == 0 else staged.at[0],
+                field_out.at[region] if kind == 0 else next_out.at[1 - region],
+                send_last.at[kind, 0], recv_last.at[kind, region], at(source),
+            ).wait_recv()
+
+    for k in (0, 1):
+        hand(0, k, True)
     sign = 2 * core - 1
     for step in range(steps):
         for d in range(1, chips):
             trace_moves[step * (chips - 1) + d - 1].wait_recv()
         shift = sign * offsets[step] + count
-        near = lax.rem(place + shift, count)
-        far = lax.rem(2 * chip + other + shift, count)
-        next_out[other, step] = whole[step][lax.div(near, 2), lax.rem(near, 2)]
-        staged[step] = whole[step][lax.div(far, 2), lax.rem(far, 2)]
-    swap_next = copy(
-        staged, next_out.at[other], send_last.at[1], recv_last.at[1], device(chip, other),
-    )
-    swap_next.start()
-    for line in moves:
-        for move in line:
-            move.wait_send()
+        for k in (0, 1):
+            near = lax.rem(2 * chip + k + shift, count)
+            staged[k, step] = whole[step][lax.div(near, 2), lax.rem(near, 2)]
+    for k in (0, 1):
+        hand(1, k, True)
+    for part in parts:
+        ship(part, False)
     for line in halo_moves:
         for move in line:
             move.wait_send()
     for move in trace_moves:
         move.wait_send()
-    swap.wait()
-    swap_next.wait()
+    for kind in (0, 1):
+        for k in (0, 1):
+            hand(kind, k, False)
+            take(kind, k)
 
 
 def per_device(
@@ -282,7 +330,7 @@
             area(steps + 1, ext),
             area(ext),
             area(2, ext),
-            pltpu.VMEM((steps, cells, axial), jnp.float32),
+            pltpu.VMEM((2, steps, cells, axial), jnp.float32),
             dma((3, 2)),
             dma((3, 2)),
             dma((3, 2)),
@@ -291,8 +339,8 @@
             dma((steps, 2)),
             dma((steps, chips)),
             dma((steps, chips)),
-            dma((2,)),
-            dma((2,)),
+            dma((2, 2)),
+            dma((2, 2)),
             *[pltpu.VMEM((chips, 2, cells, axial), jnp.float32) for _ in range(steps)],
         ],
         compiler_params=pltpu.CompilerParams(

time: 46.4 us -> 42.6 us (0.918)
  Pallas kernels: 41.7 us -> 38 us
    pallas_call x1, Pallas kernels: 41.7 us -> 38 us  [per_device(): pl.pallas_call(functools.partial(kernel, count, cells, steps, radial, axi...]
where the time goes in v2:
time: 42.6 us; the launch traced here: 42.4 us
  Pallas kernels  38 us (89%)
  local copies, waits for them, and re-layouts  3.62 us (8%)
  between operations  0.74 us (2%)
    pallas_call x1, Pallas kernels, per_device(): pl.pallas_call(functools.partial(kernel, count, cells, steps, radial, axi...  38 us
    unnamed x20, local copies, waits for them, and re-layouts  2.78 us

profile of v2, /device:TPU:0, one launch (start us, length us, event | category | flops | bytes accessed | tf_op | source)
XLA Modules:
  0.0 42.4 jit_solution(6503347479513914273)
XLA Ops:
  0.6 0.0 copy-start.6
  0.6 0.8 %copy.15 = f32[2,4,4,256]{3,2,1,0:T(4,128)S(1)} copy(f32[2,4,4,256]{3,1,2,0:T(4,128)} %bitcast.9) | data formatting | bytes 65536 | tf_op jit(solution)/shard_map/transpose | solution.py:308
  1.5 0.0 copy-done.6
  1.5 0.0 copy-start.7
  1.5 0.0 copy-start.8
  1.5 0.8 %copy-done.7 = f32[2,8,4,256]{3,2,1,0:T(4,128)S(1)} copy-done((f32[2,8,4,256]{3,2,1,0:T(4,128)S(1)}, f32[2,8,4,256]{3,2,1,0:T(4,128)}, u32[]{:S(2)}) %copy-start.7) | copy-done | bytes 65560
  2.3 0.0 copy-done.8
  2.4 0.0 copy-start
  2.4 0.0 copy-start.1
  2.4 0.0 copy-start.2
  2.4 0.0 copy-start.3
  2.4 0.0 copy-start.4
  2.4 0.0 copy-start.5
  2.5 0.6 %copy-done = f32[4]{0:T(128)S(1)} copy-done((f32[4]{0:T(128)S(1)}, f32[4]{0:T(128)}, u32[]{:S(2)}) %copy-start) | copy-done | bytes 40
  3.0 0.0 copy-done.1
  3.1 0.0 copy-done.2
  3.1 0.0 copy-done.3
  3.1 0.0 copy-done.4
  3.1 0.0 copy-done.5
  3.1 38.0 %window.1 = (f32[2,4,8,256]{3,2,1,0:T(8,128)S(1)}, f32[2,4,4,256]{3,2,1,0:T(4,128)S(1)}) custom-call(f32[4]{0:T(128)S(1)} %copy-done, s32[4]{0:T(128)S(1)} %copy-done.1, s32[4]{0:T(128)S(1)} %copy-done.2, f32[4]{0:T(128)S(1)} %copy-done.3, f32[4]{0:T(128)S(1)} %copy-done.4, f32[2]{0:T(128)S(1)} %copy-done.5, f32[2,14,8,256]{3,2,1,0:T(8,128)S(1)} %pad_maximum_fusion.packed), custom_call_target="tpu_custom_call" | custom-call | tf_op jit(solution)/shard_map/window/pallas_call | solution.py:319
  41.1 0.7 %copy.16 = f32[2,8,4,256]{3,2,1,0:T(4,128)} copy(f32[2,8,4,256]{3,1,2,0:T(8,128)S(1)} %bitcast.8) | data formatting | bytes 131072
  41.8 0.6 %copy.23 = f32[2,4,4,256]{3,2,1,0:T(4,128)} copy(f32[2,4,4,256]{3,2,1,0:T(4,128)S(1)} %get-tuple-element.13) | data formatting | bytes 65536
  (4 shorter events, 0.1 us)
Async XLA Ops:
  0.6 0.8 %copy-start.6 = (s32[2,8,4,256]{3,2,1,0:T(4,128)S(1)}, s32[2,8,4,256]{3,2,1,0:T(4,128)}, u32[]{:S(2)}) copy-start(s32[2,8,4,256]{3,2,1,0:T(4,128)} %param.12) | copy-start | bytes 196612
  1.5 0.8 %copy-start.7 = (f32[2,8,4,256]{3,2,1,0:T(4,128)S(1)}, f32[2,8,4,256]{3,2,1,0:T(4,128)}, u32[]{:S(2)}) copy-start(f32[2,8,4,256]{3,2,1,0:T(4,128)} %param.11) | copy-start | bytes 196612
  1.5 0.9 %copy-start.8 = (f32[2,8,4,256]{3,2,1,0:T(4,128)S(1)}, f32[2,8,4,256]{3,2,1,0:T(4,128)}, u32[]{:S(2)}) copy-start(f32[2,8,4,256]{3,2,1,0:T(4,128)} %param.10) | copy-start | bytes 196612
  2.4 0.7 %copy-start = (f32[4]{0:T(128)S(1)}, f32[4]{0:T(128)}, u32[]{:S(2)}) copy-start(f32[4]{0:T(128)} %waveform.1) | copy-start | bytes 52
  2.4 0.7 %copy-start.1 = (s32[4]{0:T(128)S(1)}, s32[4]{0:T(128)}, u32[]{:S(2)}) copy-start(s32[4]{0:T(128)} %degrees.1) | copy-start | bytes 52
  2.4 0.7 %copy-start.2 = (s32[4]{0:T(128)S(1)}, s32[4]{0:T(128)}, u32[]{:S(2)}) copy-start(s32[4]{0:T(128)} %offsets.1) | copy-start | bytes 52
  2.4 0.7 %copy-start.3 = (f32[4]{0:T(128)S(1)}, f32[4]{0:T(128)}, u32[]{:S(2)}) copy-start(f32[4]{0:T(128)} %conduct.1) | copy-start | bytes 52
  2.4 0.7 %copy-start.4 = (f32[4]{0:T(128)S(1)}, f32[4]{0:T(128)}, u32[]{:S(2)}) copy-start(f32[4]{0:T(128)} %reluct.1) | copy-start | bytes 52
  2.4 0.7 %copy-start.5 = (f32[2]{0:T(128)S(1)}, f32[2]{0:T(128)}, u32[]{:S(2)}) copy-start(f32[2]{0:T(128)} %robin.1) | copy-start | bytes 28
